TPU v7x, 256 devices: a whole 4x4x8 slice. The times are simulated.
256 devices in a mesh: row: 8 (over z_lo, x), col: 32 (over z_hi, y, core).
Axes of the slice: x: 4, y: 4, z: 8 (z_hi: 4, z_lo: 2; z = z_hi * 2 + z_lo), core: 2. Of those that a mesh axis runs over, the one named last changes fastest.
Arguments:
- activations: bfloat16 [262144, 896], P(('row', 'col')), may hold values from -6 to 6
- cotangent: bfloat16 [262144, 896], P(('row', 'col')), may hold values from -6 to 6
- inner_first: bfloat16 [28672, 7168], P('col', 'row'), may hold values from -6 to 6
- inner_second: bfloat16 [7168, 28672], P('row', 'col'), may hold values from -6 to 6
- outer_first: float32 [896, 7168], P('col', 'row'), may hold values from -6 to 6
- momentum_first: float32 [896, 7168], P('col', 'row'), may hold values from -3 to 3
- outer_second: float32 [896, 28672], P('row', 'col'), may hold values from -6 to 6
- momentum_second: float32 [896, 28672], P('row', 'col'), may hold values from -3 to 3
Outputs:
- new_outer_first: float32 [896, 7168], P('col', 'row')
- new_momentum_first: float32 [896, 7168], P('col', 'row')
- new_outer_second: float32 [896, 28672], P('row', 'col')
- new_momentum_second: float32 [896, 28672], P('row', 'col')
- reset_first: bfloat16 [28672, 7168], P('col', 'row')
- reset_second: bfloat16 [7168, 28672], P('row', 'col')
All inputs are finite; a program needn't handle non-finite values.
Results may differ from a plain program's by a relative error of at most 0.003.
Values may be sent and summed in bfloat16 or wider, within the bound.
No kernel may reach another device: no remote copies, remote signals or barrier semaphores. Data moves between devices by JAX's collectives and lax.ppermute only.
A program may use at most 64 MiB of HBM per device.

v0:
```python
import jax
import jax.numpy as jnp
from jax import lax
from jax.sharding import PartitionSpec as P

inner_rate = 1.0
outer_rate = 0.7
momentum_coef = 0.9


def nesterov(outer_rows, moment_rows, summed, count):
    pseudo_grad = outer_rows - summed / count
    moment_new = momentum_coef * moment_rows + pseudo_grad
    outer_new = outer_rows - outer_rate * (pseudo_grad + momentum_coef * moment_new)
    return (outer_new, moment_new)


def on_device(
    activations,
    cotangent,
    inner_first,
    inner_second,
    outer_first,
    momentum_first,
    outer_second,
    momentum_second,
):
    width = inner_first.shape[0]
    unit_scale = 1.0 / jnp.sqrt(jnp.float32(width))
    row_count = lax.axis_size("row")
    col_count = lax.axis_size("col")
    rows_second = outer_second.shape[0]
    rows_first = outer_first.shape[0]
    hidden = jnp.dot(activations, inner_first, preferred_element_type=jnp.float32) * unit_scale
    logistic = jax.nn.sigmoid(hidden)
    second_in = (hidden * logistic).astype(jnp.bfloat16)
    backward = (
        lax.dot_general(
            cotangent, inner_second, (((1,), (1,)), ((), ())), preferred_element_type=jnp.float32
        )
        * unit_scale
    )
    first_cot = (backward * logistic * (1.0 + hidden * (1.0 - logistic))).astype(jnp.bfloat16)

    def final_rows(inputs, grads, weight):
        grad_rows = (
            lax.dot_general(
                inputs, grads, (((0,), (0,)), ((), ())), preferred_element_type=jnp.float32
            )
            * unit_scale
        )
        return weight.astype(jnp.float32) - inner_rate * grad_rows

    final_second = final_rows(second_in, cotangent, inner_second)
    summed_second = lax.psum(final_second, "row")
    final_first = final_rows(activations, first_cot, inner_first)
    summed_first = lax.psum(final_first, "col")
    mine_second = lax.dynamic_slice_in_dim(
        summed_second, lax.axis_index("row") * rows_second, rows_second, 0
    )
    mine_first = lax.dynamic_slice_in_dim(
        summed_first, lax.axis_index("col") * rows_first, rows_first, 0
    )
    new_outer_second, new_momentum_second = nesterov(
        outer_second, momentum_second, mine_second, row_count
    )
    new_outer_first, new_momentum_first = nesterov(
        outer_first, momentum_first, mine_first, col_count
    )
    reset_second = lax.all_gather(new_outer_second.astype(jnp.bfloat16), "row", axis=0, tiled=True)
    reset_first = lax.all_gather(new_outer_first.astype(jnp.bfloat16), "col", axis=0, tiled=True)
    return (
        new_outer_first,
        new_momentum_first,
        new_outer_second,
        new_momentum_second,
        reset_first,
        reset_second,
    )


def solution(mesh):
    return jax.shard_map(
        on_device,
        mesh=mesh,
        in_specs=(
            P(("row", "col"), None),
            P(("row", "col"), None),
            P("col", "row"),
            P("row", "col"),
            P("col", "row"),
            P("col", "row"),
            P("row", "col"),
            P("row", "col"),
        ),
        out_specs=(
            P("col", "row"),
            P("col", "row"),
            P("row", "col"),
            P("row", "col"),
            P("col", "row"),
            P("row", "col"),
        ),
        check_vma=False,
    )
```

profile of v0, /device:TPU:1, one launch (start us, length us, event | category | flops | bytes accessed | tf_op | source)
XLA Modules:
  0.0 529.3 jit_solution(17017772558369604496)
XLA Ops:
  7.2 0.0 copy-start
  7.2 0.0 all-reduce.5.cloned.1.call-start
  7.2 3.0 copy.44
  10.3 0.0 copy-done
  10.3 0.0 copy-start.6
  10.3 3.8 fusion.6
  14.1 0.0 copy-start.7
  14.1 1.8 copy-done.7
  15.9 0.0 copy-done.6
  15.9 4.1 multiply_subtract_fusion
  20.0 0.0 copy-start.1
  20.0 0.0 all-reduce.5.cloned.1.call-update
  20.0 0.0 all-reduce.3.cloned.1.call-start
  20.1 1.3 copy-done.1
  21.4 9.3 %bitcast_subtract_fusion = f32[896,896]{1,0:T(8,128)} fusion(bf16[896,896]{1,0:T(8,128)(2,1)} %param.10, bf16[1024,896]{1,0:T(8,128)(2,1)S(1)} %copy-done, f32[1024,896]{1,0:T(8,128)} %copy-done.7, bf16[1024,896]{1,0:T(8,128)(2,1)} %param.9, bf16[896,896]{1,0:T(8,128)(2,1)S(1)} %copy-done.1), kind=kOutput, calls=%fused_computation.3 | convolution fusion | flops 3300835328 | bytes 13762560 | tf_op jit(solution)/shard_map/dot_general | solution.py:47
  30.7 0.0 copy-start.3
  30.7 0.0 copy-start.4
  30.7 0.0 all-reduce.3.cloned.1.call-update
  30.8 0.0 copy-start.5
  30.8 0.0 all-gather.4.cloned.1.call-start
  30.8 0.9 copy-done.3
  31.7 0.2 copy.48
  31.9 0.0 copy-done.4
  32.0 1.0 copy.47
  32.9 85.0 %all-reduce.5.cloned.1.call-done = f32[896,896]{0,1:T(8,128)} async-done(((f32[896,896]{0,1:T(8,128)}), f32[896,896]{0,1:T(8,128)}) %all-reduce.5.cloned.1.call-update) | async-done | bytes 3211280 | tf_op jit(solution)/shard_map/psum | solution.py:55
  117.9 1.5 fusion.5
  119.4 0.8 copy.49
  120.3 0.0 all-gather.4.cloned.1.call-update
  120.3 0.0 all-gather.6.cloned.1.call-start
  120.3 295.8 %all-reduce.3.cloned.1.call-done = f32[896,896]{1,0:T(8,128)} async-done(((f32[896,896]{1,0:T(8,128)}), f32[896,896]{1,0:T(8,128)}) %all-reduce.3.cloned.1.call-update) | async-done | bytes 3211280 | tf_op jit(solution)/shard_map/psum | solution.py:57
  416.1 0.0 copy-done.5
  416.1 1.7 convert_bitcast_fusion
  417.8 0.0 all-gather.6.cloned.1.call-update
  417.9 0.9 copy.50
  418.8 0.9 copy.51
  419.8 35.5 %all-gather.4.cloned.1.call-done = bf16[896,896]{1,0:T(8,128)(2,1)} async-done(((bf16[112,896]{1,0:T(8,128)(2,1)}), bf16[896,896]{1,0:T(8,128)(2,1)}) %all-gather.4.cloned.1.call-update) | async-done | bytes 1605648 | tf_op jit(solution)/shard_map/all_gather | solution.py:70
  455.3 0.0 copy-start.2
  455.3 62.8 %all-gather.6.cloned.1.call-done = bf16[32,28,896]{2,1,0:T(8,128)(2,1)} async-done(((bf16[1,28,896]{2,1,0:T(8,128)(2,1)}), bf16[32,28,896]{2,1,0:T(8,128)(2,1)}) %all-gather.6.cloned.1.call-update) | async-done | bytes 1605648 | tf_op jit(solution)/shard_map/all_gather | solution.py:71
  518.0 3.5 reshape.13
  521.6 0.0 copy-done.2
  521.6 1.2 copy.57
Async XLA Ops:
  7.2 3.1 copy-start
  7.2 110.7 %all-reduce.5.cloned.1.call-start = ((), (), s32[]{:S(2)}) async-start(), calls=%async_computation.1 | async-start | bytes 6422528 | tf_op jit(solution)/shard_map/psum | solution.py:55
  10.3 5.6 %copy-start.6 = (bf16[1024,896]{1,0:T(8,128)(2,1)S(1)}, bf16[1024,896]{1,0:T(8,128)(2,1)}, u32[]{:S(2)}) copy-start(bf16[1024,896]{1,0:T(8,128)(2,1)} %param.9) | copy-start | bytes 5505028
  14.1 1.8 copy-start.7
  20.0 1.4 copy-start.1
  20.0 396.1 %all-reduce.3.cloned.1.call-start = ((), (), s32[]{:S(2)}) async-start(), calls=%async_computation | async-start | bytes 6422528 | tf_op jit(solution)/shard_map/psum | solution.py:57
  30.7 1.0 copy-start.3
  30.7 1.2 copy-start.4
  30.8 385.4 %copy-start.5 = (f32[28,896]{1,0:T(8,128)S(1)}, f32[28,896]{1,0:T(8,128)}, u32[]{:S(2)}) copy-start(f32[28,896]{1,0:T(8,128)} %param.12) | copy-start | bytes 301060
  30.8 424.5 %all-gather.4.cloned.1.call-start = ((), (), s32[]{:S(2)}) async-start(), calls=%async_computation.2 | async-start | bytes 1806336 | tf_op jit(solution)/shard_map/all_gather | solution.py:70
  120.3 397.7 %all-gather.6.cloned.1.call-start = ((), (), s32[]{:S(2)}) async-start(), calls=%async_computation.3 | async-start | bytes 1892352 | tf_op jit(solution)/shard_map/all_gather | solution.py:71
  455.3 66.3 %copy-start.2 = (bf16[896,896]{1,0:T(8,128)(2,1)S(1)}, bf16[896,896]{1,0:T(8,128)(2,1)}, u32[]{:S(2)}) copy-start(bf16[896,896]{1,0:T(8,128)(2,1)} %all-gather.4.cloned.1.call-done) | copy-start | bytes 4816900
Sparse Core Ops, SparseCore 0:
  20.1 97.7 all-reduce.4
  120.6 295.4 all-reduce.2
  418.6 36.5 all-gather.3
  458.6 59.4 all-gather.5
where the time goes:
time: 530 us; the launch traced here: 529 us
  waiting for transfers between devices  479 us (90%)
  matrix products  17.2 us (3%)
  local copies, waits for them, and re-layouts  15.7 us (3%)
  between operations  13.9 us (3%)
    psum x1, waiting for transfers between devices, on_device(): summed_first = lax.psum(final_first, 'col')  296 us
    psum x1, waiting for transfers between devices, on_device(): summed_second = lax.psum(final_second, 'row')  85 us
    all_gather x1, waiting for transfers between devices, on_device(): lax.all_gather(new_outer_first.astype(jnp.bfloat16), 'col', axis=0, tiled...  62.8 us
    all_gather x1, waiting for transfers between devices, on_device(): lax.all_gather(new_outer_second.astype(jnp.bfloat16), 'row', axis=0, tile...  35.5 us
    unnamed x23, local copies, waits for them, and re-layouts  14.9 us
    dot_general x2, matrix products, final_rows(): lax.dot_general(inputs, grads, (((0,), (0,)), ((), ())), preferred_elemen...  13.4 us
  transfers between devices with their start and end apart: 4, of which 4 were waited for; matrix products, arithmetic and copies ran while one was open for 3% of the time, Pallas kernels for 0%

commit v1 on v0

--- a/solution.py
+++ b/solution.py
@@ -6,6 +6,10 @@
 inner_rate = 1.0
 outer_rate = 0.7
 momentum_coef = 0.9
+
+ROWS, COLS = 8, 32
+CORE_SWAP = [(i, i ^ 1) for i in range(COLS)]
+CHIP_GROUPS = [[2 * k + c for k in range(COLS // 2)] for c in range(2)]
 
 
 def nesterov(outer_rows, moment_rows, summed, count):
@@ -27,10 +31,9 @@
 ):
     width = inner_first.shape[0]
     unit_scale = 1.0 / jnp.sqrt(jnp.float32(width))
-    row_count = lax.axis_size("row")
-    col_count = lax.axis_size("col")
     rows_second = outer_second.shape[0]
     rows_first = outer_first.shape[0]
+    core = lax.axis_index("col") % 2
     hidden = jnp.dot(activations, inner_first, preferred_element_type=jnp.float32) * unit_scale
     logistic = jax.nn.sigmoid(hidden)
     second_in = (hidden * logistic).astype(jnp.bfloat16)
@@ -51,24 +54,49 @@
         )
         return weight.astype(jnp.float32) - inner_rate * grad_rows
 
-    final_second = final_rows(second_in, cotangent, inner_second)
-    summed_second = lax.psum(final_second, "row")
     final_first = final_rows(activations, first_cot, inner_first)
-    summed_first = lax.psum(final_first, "col")
-    mine_second = lax.dynamic_slice_in_dim(
-        summed_second, lax.axis_index("row") * rows_second, rows_second, 0
+    pairs = final_first.reshape(COLS // 2, 2, rows_first, width)
+    mine = jnp.where(core == 0, pairs[:, 0], pairs[:, 1])
+    theirs = jnp.where(core == 0, pairs[:, 1], pairs[:, 0])
+    got = lax.ppermute(theirs, "col", CORE_SWAP)
+    chip_first = (mine + got).astype(jnp.bfloat16)
+
+    final_second = final_rows(second_in, cotangent, inner_second).astype(jnp.bfloat16)
+    terms_second = lax.all_to_all(
+        final_second.reshape(ROWS, rows_second, width), "row", 0, 0
     )
-    mine_first = lax.dynamic_slice_in_dim(
-        summed_first, lax.axis_index("col") * rows_first, rows_first, 0
+    summed_second = jnp.sum(terms_second.astype(jnp.float32), axis=0)
+    new_outer_second, new_momentum_second = nesterov(
+        outer_second, momentum_second, summed_second, ROWS
     )
-    new_outer_second, new_momentum_second = nesterov(
-        outer_second, momentum_second, mine_second, row_count
+
+    terms_first = lax.all_to_all(chip_first, "col", 0, 0, axis_index_groups=CHIP_GROUPS)
+    summed_first = jnp.sum(terms_first.astype(jnp.float32), axis=0)
+    new_outer_first, new_momentum_first = nesterov(
+        outer_first, momentum_first, summed_first, COLS
     )
-    new_outer_first, new_momentum_first = nesterov(
-        outer_first, momentum_first, mine_first, col_count
+
+    reset_second = lax.all_to_all(
+        jnp.broadcast_to(
+            new_outer_second.astype(jnp.bfloat16)[None], (ROWS, rows_second, width)
+        ),
+        "row",
+        0,
+        0,
+    ).reshape(width, width)
+    half = lax.all_to_all(
+        jnp.broadcast_to(
+            new_outer_first.astype(jnp.bfloat16)[None], (COLS // 2, rows_first, width)
+        ),
+        "col",
+        0,
+        0,
+        axis_index_groups=CHIP_GROUPS,
     )
-    reset_second = lax.all_gather(new_outer_second.astype(jnp.bfloat16), "row", axis=0, tiled=True)
-    reset_first = lax.all_gather(new_outer_first.astype(jnp.bfloat16), "col", axis=0, tiled=True)
+    other = lax.ppermute(half, "col", CORE_SWAP)
+    even = jnp.where(core == 0, half, other)
+    odd = jnp.where(core == 0, other, half)
+    reset_first = jnp.stack([even, odd], axis=1).reshape(width, width)
     return (
         new_outer_first,
         new_momentum_first,

time: 530 us -> 157 us (0.30)
  waiting for transfers between devices: 479 us -> 61.3 us
  starting transfers between devices: 0.16 us -> 36.9 us
  between operations: 13.9 us -> 0.74 us
  local copies, waits for them, and re-layouts: 15.7 us -> 25.8 us
  other arithmetic: 3.23 us -> 10.3 us
    psum x2 -> x0, waiting for transfers between devices: 381 us -> none  [the longest x1 296 us: on_device(): summed_first = lax.psum(final_first, 'col')]
    all_gather x2 -> x0, waiting for transfers between devices: 98.3 us -> none  [the longest x1 62.8 us: on_device(): lax.all_gather(new_outer_first.astype(jnp.bfloat16), 'col', axis=0, tiled...]
    all_to_all x0 -> x4, waiting for transfers between devices: none -> 56.3 us  [the longest x1 17.9 us: on_device(): lax.all_to_all(final_second.reshape(ROWS, rows_second, width), 'row', 0, 0)]
    all_to_all x0 -> x4, starting transfers between devices: none -> 32.4 us  [the longest x1 11.8 us: on_device(): lax.all_to_all(jnp.broadcast_to(new_outer_second.astype(jnp.bfloat16)[Non...]
    reshape x0 -> x2, local copies, waits for them, and re-layouts: none -> 8.12 us  [the longest x1 4.57 us: on_device(): pairs = final_first.reshape(COLS // 2, 2, rows_first, width)]
    unnamed x23 -> x16, local copies, waits for them, and re-layouts: 14.9 us -> 9.11 us
  transfers between devices with their start and end apart: 4 -> 6, of which waited for: 4 -> 6; matrix products, arithmetic and copies ran while one was open for 3% -> 16% of each run, Pallas kernels for 0% -> 0%
where the time goes in v1:
time: 157 us; the launch traced here: 156 us
  waiting for transfers between devices  61.3 us (39%)
  starting transfers between devices  36.9 us (24%)
  local copies, waits for them, and re-layouts  25.8 us (16%)
  matrix products  21.5 us (14%)
  other arithmetic  10.3 us (7%)
    all_to_all x1, waiting for transfers between devices, on_device(): lax.all_to_all(final_second.reshape(ROWS, rows_second, width), 'row', 0, 0)  17.9 us
    all_to_all x1, waiting for transfers between devices, on_device(): lax.all_to_all(jnp.broadcast_to(new_outer_first.astype(jnp.bfloat16)[None...  16.4 us
    dot_general x2, matrix products, final_rows(): lax.dot_general(inputs, grads, (((0,), (0,)), ((), ())), preferred_elemen...  15.9 us
    all_to_all x1, waiting for transfers between devices, on_device(): lax.all_to_all(jnp.broadcast_to(new_outer_second.astype(jnp.bfloat16)[Non...  12 us
    all_to_all x1, starting transfers between devices, on_device(): lax.all_to_all(jnp.broadcast_to(new_outer_second.astype(jnp.bfloat16)[Non...  11.8 us
    all_to_all x1, waiting for transfers between devices, on_device(): lax.all_to_all(chip_first, 'col', 0, 0, axis_index_groups=CHIP_GROUPS)  10.1 us
    all_to_all x1, starting transfers between devices, on_device(): lax.all_to_all(chip_first, 'col', 0, 0, axis_index_groups=CHIP_GROUPS)  9.18 us
    unnamed x16, local copies, waits for them, and re-layouts  9.11 us
  transfers between devices with their start and end apart: 6, of which 6 were waited for; matrix products, arithmetic and copies ran while one was open for 16% of the time, Pallas kernels for 0%

profile of v1, /device:TPU:1, one launch (start us, length us, event | category | flops | bytes accessed | tf_op | source)
XLA Modules:
  0.0 156.5 jit_solution(17816808213290695179)
XLA Ops:
  0.6 0.0 copy-start
  0.7 1.5 copy-done
  2.1 0.0 copy-start.4
  2.1 5.6 %fusion.8 = f32[1024,896]{1,0:T(8,128)} fusion(bf16[1024,896]{1,0:T(8,128)(2,1)S(1)} %copy-done, bf16[896,896]{1,0:T(8,128)(2,1)} %param.10), kind=kOutput, calls=%fused_computation.26 | convolution fusion | flops 1644167168 | bytes 7110656 | tf_op jit(solution)/shard_map/dot_general | solution.py:37
  7.7 0.0 copy-done.4
  7.7 9.4 %bitcast_subtract_fusion = f32[896,896]{1,0:T(8,128)} fusion(bf16[896,896]{1,0:T(8,128)(2,1)} %param.10, bf16[1024,896]{1,0:T(8,128)(2,1)S(1)} %copy-done, f32[1024,896]{1,0:T(8,128)} %fusion.8, bf16[1024,896]{1,0:T(8,128)(2,1)} %param.9, bf16[896,896]{1,0:T(8,128)(2,1)S(1)} %copy-done.4), kind=kOutput, calls=%fused_computation.3 | convolution fusion | flops 3300835328 | bytes 13762560 | tf_op jit(solution)/shard_map/dot_general | solution.py:50
  17.2 4.6 %reshape.30 = f32[16,2,28,896]{3,2,1,0:T(8,128)} reshape(f32[896,896]{1,0:T(8,128)} %bitcast_subtract_fusion) | data formatting | bytes 6422528 | tf_op jit(solution)/shard_map/reshape | solution.py:58
  21.7 0.0 copy-start.1
  21.7 2.4 %select_bitcast_fusion = f32[16,28,896]{2,1,0:T(8,128)S(1)} fusion(f32[16,2,28,896]{3,2,1,0:T(8,128)} %reshape.30, pred[]{:T(512)S(6)} %eq.4), kind=kLoop, calls=%fused_computation.10 | loop fusion | flops 401408 | bytes 4816897 | tf_op jit(solution)/shard_map/jit(_where)/select_n | solution.py:60
  24.2 0.9 copy.35
  25.1 3.3 %collective-permute-start = (f32[16,28,896]{2,0,1:T(8,128)S(1)}, f32[16,28,896]{2,0,1:T(8,128)S(1)}, u32[]{:S(2)}, u32[]{:S(2)}) collective-permute-start(f32[16,28,896]{2,0,1:T(8,128)S(1)} %copy.35), channel_id=1, source_target_pairs={{0,1},{1,0},{2,3},{3,2},{4,5},{5,4},{6,7},{7,6},{8,9},{9,8},{10,11... | collective-permute-start | bytes 4816904 | tf_op jit(solution)/shard_map/ppermute | solution.py:61
  28.4 3.1 %collective-permute-done = f32[16,28,896]{2,0,1:T(8,128)S(1)} collective-permute-done((f32[16,28,896]{2,0,1:T(8,128)S(1)}, f32[16,28,896]{2,0,1:T(8,128)S(1)}, u32[]{:S(2)}, u32[]{:S(2)}) %collective-permute-start) | collective-permute-done | bytes 1605664 | tf_op jit(solution)/shard_map/ppermute | solution.py:61
  31.5 0.0 copy-done.1
  31.5 1.5 fusion
  33.1 9.2 %all-to-all-start = ((bf16[16,28,896]{2,1,0:T(8,128)(2,1)}), bf16[16,28,896]{2,1,0:T(8,128)(2,1)S(1)}, u32[]{:S(2)}, u32[]{:S(2)}) async-start(bf16[16,28,896]{2,1,0:T(8,128)(2,1)} %fusion), calls=%async_computation | async-start | bytes 1835008 | tf_op jit(solution)/shard_map/all_to_all | solution.py:73
  42.3 3.6 %copy.37 = bf16[896,896]{0,1:T(8,128)(2,1)} copy(bf16[896,896]{1,0:T(8,128)(2,1)} %param.11) | data formatting | bytes 3211264 | tf_op args[3]
  45.8 6.5 %subtract_convert_fusion = bf16[896,896]{0,1:T(8,128)(2,1)} fusion(bf16[896,896]{0,1:T(8,128)(2,1)} %copy.37, bf16[1024,896]{1,0:T(8,128)(2,1)} %param.9, f32[1024,896]{1,0:T(8,128)} %fusion.8), kind=kOutput, calls=%fused_computation.5 | convolution fusion | flops 1652883456 | bytes 8716288 | tf_op jit(solution)/shard_map/dot_general | solution.py:50
  52.3 3.6 %copy.39 = bf16[896,896]{1,0:T(8,128)(2,1)} copy(bf16[896,896]{0,1:T(8,128)(2,1)} %subtract_convert_fusion) | data formatting | bytes 3211264 | tf_op jit(solution)/shard_map/convert_element_type | solution.py:64
  55.9 10.1 %all-to-all-done = bf16[16,28,896]{2,1,0:T(8,128)(2,1)S(1)} async-done(((bf16[16,28,896]{2,1,0:T(8,128)(2,1)}), bf16[16,28,896]{2,1,0:T(8,128)(2,1)S(1)}, u32[]{:S(2)}, u32[]{:S(2)}) %all-to-all-start) | async-done | bytes 802848 | tf_op jit(solution)/shard_map/all_to_all | solution.py:73
  65.9 0.0 copy-start.3
  65.9 0.9 copy-done.3
  66.9 6.9 %all-to-all-start.1 = ((bf16[8,112,896]{2,1,0:T(8,128)(2,1)}), bf16[8,112,896]{2,1,0:T(8,128)(2,1)S(1)}, u32[]{:S(2)}, u32[]{:S(2)}) async-start(bf16[8,112,896]{2,1,0:T(8,128)(2,1)} %bitcast.20), calls=%async_computation.1 | async-start | bytes 3211264 | tf_op jit(solution)/shard_map/all_to_all | solution.py:65
  73.8 1.3 convert_reduce_fusion.1
  75.1 1.7 %fusion.7 = (bf16[28,896]{1,0:T(8,128)(2,1)S(1)}, f32[28,896]{1,0:T(8,128)}, f32[28,896]{1,0:T(8,128)}) fusion(f32[28,896]{1,0:T(8,128)} %param.12, f32[28,896]{1,0:T(8,128)S(1)} %convert_reduce_fusion.1, f32[28,896]{1,0:T(8,128)} %param.13), kind=kLoop, calls=%fused_computation.25 | loop fusion | flops 225792 | bytes 551936 | tf_op jit(solution)/shard_map/convert_element_type | solution.py:89
  76.8 17.9 %all-to-all-done.1 = bf16[8,112,896]{2,1,0:T(8,128)(2,1)S(1)} async-done(((bf16[8,112,896]{2,1,0:T(8,128)(2,1)}), bf16[8,112,896]{2,1,0:T(8,128)(2,1)S(1)}, u32[]{:S(2)}, u32[]{:S(2)}) %all-to-all-start.1) | async-done | bytes 1605664 | tf_op jit(solution)/shard_map/all_to_all | solution.py:65
  94.6 0.0 copy-start.2
  94.6 1.0 broadcast_in_dim.4
  95.7 0.4 copy-done.2
  96.1 4.5 %all-to-all-start.2 = ((bf16[16,28,896]{2,1,0:T(8,128)(2,1)}), bf16[16,28,896]{2,1,0:T(8,128)(2,1)S(1)}, u32[]{:S(2)}, u32[]{:S(2)}) async-start(bf16[16,28,896]{2,1,0:T(8,128)(2,1)} %broadcast_in_dim.4), calls=%async_computation.2 | async-start | bytes 1835008 | tf_op jit(solution)/shard_map/all_to_all | solution.py:87
  100.6 0.0 copy-start.5
  100.6 0.0 copy-start.6
  100.7 1.7 %convert_reduce_fusion = f32[112,896]{1,0:T(8,128)S(1)} fusion(bf16[8,112,896]{2,1,0:T(8,128)(2,1)} %copy-done.2), kind=kLoop, calls=%fused_computation.4 | loop fusion | flops 1505280 | bytes 2007040 | tf_op jit(solution)/shard_map/reduce_sum | solution.py:68
  102.4 0.0 copy-done.5
  102.4 0.0 copy-done.6
  102.4 1.0 fusion.6
  103.4 16.4 %all-to-all-done.2 = bf16[16,28,896]{2,1,0:T(8,128)(2,1)S(1)} async-done(((bf16[16,28,896]{2,1,0:T(8,128)(2,1)}), bf16[16,28,896]{2,1,0:T(8,128)(2,1)S(1)}, u32[]{:S(2)}, u32[]{:S(2)}) %all-to-all-start.2) | async-done | bytes 802848 | tf_op jit(solution)/shard_map/all_to_all | solution.py:87
  119.8 1.3 broadcast_in_dim.5
  121.1 11.8 %all-to-all-start.3 = ((bf16[8,112,896]{2,1,0:T(8,128)(2,1)}), bf16[8,112,896]{2,1,0:T(8,128)(2,1)}, u32[]{:S(2)}, u32[]{:S(2)}) async-start(bf16[8,112,896]{2,1,0:T(8,128)(2,1)} %broadcast_in_dim.5), calls=%async_computation.3 | async-start | bytes 3211264 | tf_op jit(solution)/shard_map/all_to_all | solution.py:79
  132.8 0.2 copy.40
  133.1 1.2 collective-permute-start.1
  134.2 1.9 %collective-permute-done.1 = bf16[16,28,896]{2,0,1:T(8,128)(2,1)S(1)} collective-permute-done((bf16[16,28,896]{2,0,1:T(8,128)(2,1)S(1)}, bf16[16,28,896]{2,0,1:T(8,128)(2,1)S(1)}, u32[]{:S(2)}, u32[]{:S(2)}) %collective-permute-start.1) | collective-permute-done | bytes 802848 | tf_op jit(solution)/shard_map/ppermute | solution.py:96
  136.2 0.3 select_bitcast_fusion.2
  136.4 0.3 pad_maximum_fusion
  136.7 1.5 copy.43
  138.2 3.5 %reshape.32 = bf16[896,896]{1,0:T(8,128)(2,1)} reshape(bf16[16,2,28,896]{3,2,1,0:T(8,128)(2,1)} %copy.43) | data formatting | bytes 3211264 | tf_op jit(solution)/shard_map/reshape | solution.py:99
  141.8 12.0 %all-to-all-done.3 = bf16[8,112,896]{2,1,0:T(8,128)(2,1)} async-done(((bf16[8,112,896]{2,1,0:T(8,128)(2,1)}), bf16[8,112,896]{2,1,0:T(8,128)(2,1)}, u32[]{:S(2)}, u32[]{:S(2)}) %all-to-all-start.3) | async-done | bytes 1605664 | tf_op jit(solution)/shard_map/all_to_all | solution.py:79
  153.8 2.7 %copy.49 = bf16[896,896]{1,0:T(8,128)(2,1)} copy(bf16[896,896]{1,0:T(8,128)(2,1)} %bitcast.6) | data formatting | bytes 3211264
Async XLA Ops:
  0.6 1.5 copy-start
  2.1 5.6 %copy-start.4 = (bf16[896,896]{1,0:T(8,128)(2,1)S(1)}, bf16[896,896]{1,0:T(8,128)(2,1)}, u32[]{:S(2)}) copy-start(bf16[896,896]{1,0:T(8,128)(2,1)} %param.11) | copy-start | bytes 4816900
  21.7 9.8 %copy-start.1 = (f32[16,2,28,896]{3,2,1,0:T(8,128)S(1)}, f32[16,2,28,896]{3,2,1,0:T(8,128)}, u32[]{:S(2)}) copy-start(f32[16,2,28,896]{3,2,1,0:T(8,128)} %reshape.30) | copy-start | bytes 9633796
  25.1 6.4 %collective-permute-start = (f32[16,28,896]{2,0,1:T(8,128)S(1)}, f32[16,28,896]{2,0,1:T(8,128)S(1)}, u32[]{:S(2)}, u32[]{:S(2)}) collective-permute-start(f32[16,28,896]{2,0,1:T(8,128)S(1)} %copy.35), channel_id=1, source_target_pairs={{0,1},{1,0},{2,3},{3,2},{4,5},{5,4},{6,7},{7,6},{8,9},{9,8},{10,11... | collective-permute-start | bytes 4816904 | tf_op jit(solution)/shard_map/ppermute | solution.py:61
  33.1 32.9 %all-to-all-start = ((bf16[16,28,896]{2,1,0:T(8,128)(2,1)}), bf16[16,28,896]{2,1,0:T(8,128)(2,1)S(1)}, u32[]{:S(2)}, u32[]{:S(2)}) async-start(bf16[16,28,896]{2,1,0:T(8,128)(2,1)} %fusion), calls=%async_computation | async-start | bytes 1835008 | tf_op jit(solution)/shard_map/all_to_all | solution.py:73
  65.9 0.9 copy-start.3
  66.9 27.8 %all-to-all-start.1 = ((bf16[8,112,896]{2,1,0:T(8,128)(2,1)}), bf16[8,112,896]{2,1,0:T(8,128)(2,1)S(1)}, u32[]{:S(2)}, u32[]{:S(2)}) async-start(bf16[8,112,896]{2,1,0:T(8,128)(2,1)} %bitcast.20), calls=%async_computation.1 | async-start | bytes 3211264 | tf_op jit(solution)/shard_map/all_to_all | solution.py:65
  94.6 1.5 copy-start.2
  96.1 23.7 %all-to-all-start.2 = ((bf16[16,28,896]{2,1,0:T(8,128)(2,1)}), bf16[16,28,896]{2,1,0:T(8,128)(2,1)S(1)}, u32[]{:S(2)}, u32[]{:S(2)}) async-start(bf16[16,28,896]{2,1,0:T(8,128)(2,1)} %broadcast_in_dim.4), calls=%async_computation.2 | async-start | bytes 1835008 | tf_op jit(solution)/shard_map/all_to_all | solution.py:87
  100.6 1.8 %copy-start.5 = (f32[112,896]{1,0:T(8,128)S(1)}, f32[112,896]{1,0:T(8,128)}, u32[]{:S(2)}) copy-start(f32[112,896]{1,0:T(8,128)} %param.14) | copy-start | bytes 1204228
  100.6 1.8 %copy-start.6 = (f32[112,896]{1,0:T(8,128)S(1)}, f32[112,896]{1,0:T(8,128)}, u32[]{:S(2)}) copy-start(f32[112,896]{1,0:T(8,128)} %param.15) | copy-start | bytes 1204228
  121.1 32.7 %all-to-all-start.3 = ((bf16[8,112,896]{2,1,0:T(8,128)(2,1)}), bf16[8,112,896]{2,1,0:T(8,128)(2,1)}, u32[]{:S(2)}, u32[]{:S(2)}) async-start(bf16[8,112,896]{2,1,0:T(8,128)(2,1)} %broadcast_in_dim.5), calls=%async_computation.3 | async-start | bytes 3211264 | tf_op jit(solution)/shard_map/all_to_all | solution.py:79
  133.1 3.1 %collective-permute-start.1 = (bf16[16,28,896]{2,0,1:T(8,128)(2,1)S(1)}, bf16[16,28,896]{2,0,1:T(8,128)(2,1)S(1)}, u32[]{:S(2)}, u32[]{:S(2)}) collective-permute-start(bf16[16,28,896]{2,0,1:T(8,128)(2,1)S(1)} %copy.40), channel_id=1, source_target_pairs={{0,1},{1,0},{2,3},{3,2},{4,5},{5,4},{6,7},{7,6},{8,9},{9,8},{10,11... | collective-permute-start | bytes 2408456 | tf_op jit(solution)/shard_map/ppermute | solution.py:96

commit v2 on v0

v2 whole, which is shorter than its diff:
```python
import jax
import jax.numpy as jnp
from jax import lax
from jax.experimental import pallas as pl
from jax.experimental.pallas import tpu as pltpu
from jax.sharding import PartitionSpec as P

F32, BF16 = jnp.float32, jnp.bfloat16
inner_rate = 1.0
outer_rate = 0.7
momentum_coef = 0.9

T, D = 1024, 896
ROWS, COLS = 8, 32
ZL, XS = 2, 4
ZS, YS, CORES = 4, 4, 2
SUB = D // COLS
BLK = ZS * SUB
SUB2 = D // ROWS
TB = 512
RB = 448
X_GROUPS = [[z * XS + x for x in range(XS)] for z in range(ZL)]
UNIT = 1.0 / float(D) ** 0.5
VMEM_BYTES = 32 * 2**20
MOST_VMEM = 60 * 2**20


def shift(dz, dy, dc):
    def index(z, y, c):
        return ((z % ZS) * YS + y % YS) * CORES + c % CORES

    return [
        (index(z, y, c), index(z + dz, y + dy, c + dc))
        for z in range(ZS)
        for y in range(YS)
        for c in range(CORES)
    ]


def dot(a, b, ca, cb):
    return lax.dot_general(a, b, (((ca,), (cb,)), ((), ())), preferred_element_type=F32)


def place():
    col, row = lax.axis_index("col"), lax.axis_index("row")
    y = lax.rem(col // CORES, YS)
    return (col // (YS * CORES), y, lax.rem(col, CORES), row // XS)


def pick(position, options):
    value = options[0]
    for i in range(1, len(options)):
        value = jnp.where(position == i, options[i], value)
    return value


def nesterov(outer_rows, moment_rows, summed, count):
    pseudo_grad = outer_rows - summed / count
    moment_new = momentum_coef * moment_rows + pseudo_grad
    outer_new = outer_rows - outer_rate * (pseudo_grad + momentum_coef * moment_new)
    return (outer_new, moment_new)


def terms_kernel(x_hbm, w1_hbm, g_hbm, w2_hbm, mine, theirs, second, x, w1, g, w2, s, fc, acc, sems):
    def fetch(src, dst, i):
        return pltpu.make_async_copy(src, dst, sems.at[i])

    steps = T // TB
    parts = [pl.ds(t * TB, TB) for t in range(steps)]
    get_w1, get_w2 = fetch(w1_hbm, w1, 0), fetch(w2_hbm, w2, 1)
    get_x = [fetch(x_hbm.at[p], x.at[p], 2 + t) for t, p in enumerate(parts)]
    get_g = [fetch(g_hbm.at[p], g.at[p], 2 + steps + t) for t, p in enumerate(parts)]
    for copy in [get_x[0], get_w1, get_g[0], get_w2]:
        copy.start()
    for t in range(1, steps):
        get_x[t].start()
        get_g[t].start()
    for t, rows in enumerate(parts):
        if t == 0:
            get_w1.wait()
        get_x[t].wait()
        hidden = dot(x[rows, :], w1[...], 1, 0) * UNIT
        logistic = 0.5 * jnp.tanh(0.5 * hidden) + 0.5
        s[rows, :] = (hidden * logistic).astype(BF16)
        if t == 0:
            get_w2.wait()
        get_g[t].wait()
        backward = dot(g[rows, :], w2[...], 1, 1) * UNIT
        fc[rows, :] = (backward * logistic * (1.0 + hidden * (1.0 - logistic))).astype(BF16)
    for r in range(D // RB):
        cols = pl.ds(r * RB, RB)
        acc[cols, :] = w1[cols, :].astype(F32) - inner_rate * UNIT * dot(x[:, cols], fc[...], 0, 0)
        grad_second = UNIT * dot(s[:, cols], g[...], 0, 0)
        second[cols, :] = (w2[cols, :].astype(F32) - inner_rate * grad_second).astype(BF16)
    core = place()[2]
    for z in range(ZS):
        for y in range(YS):
            first = (z * YS + y) * CORES * SUB
            even = acc[pl.ds(first, SUB), :]
            odd = acc[pl.ds(first + SUB, SUB), :]
            rows = pl.ds(BLK * y + SUB * z, SUB)
            mine[rows, :] = jnp.where(core == 0, even, odd)
            theirs[rows, :] = jnp.where(core == 0, odd, even)


def core_sum_kernel(mine, got, own, *sends):
    y = place()[1]
    for k in range(YS):
        rows = pl.ds(pl.multiple_of(lax.rem(y + k, YS) * BLK, 16), BLK)
        block = mine[rows, :] + got[rows, :]
        if k == 0:
            own[...] = block
        else:
            sends[k - 1][...] = block.astype(BF16)


def y_sum_kernel(own, r1, r2, r3, total, o0, o1, o2, o3):
    z = place()[0]
    total[...] = own[...] + r1[...].astype(F32) + r2[...].astype(F32) + r3[...].astype(F32)
    for k, out in enumerate((o0, o1, o2, o3)):
        piece = pick(lax.rem(z + k, ZS), [total[pl.ds(SUB * j, SUB), :] for j in range(ZS)])
        out[...] = piece.astype(out.dtype)


def update_first_kernel(a, b, c, d, outer, moment, new_outer, new_moment, low):
    summed = a[...] + b[...] + c[...].astype(F32) + d[...]
    outer_new, moment_new = nesterov(outer[...], moment[...], summed, ROWS * YS)
    new_outer[...] = outer_new
    new_moment[...] = moment_new
    low[...] = outer_new.astype(BF16)


def join_z_kernel(p0, p1, p2, p3, out, wide):
    z = place()[0]
    pieces = [p[...].astype(F32) for p in (p0, p1, p2, p3)]
    for j in range(ZS):
        wide[pl.ds(SUB * j, SUB), :] = pick(lax.rem(z - j + ZS, ZS), pieces)
    out[...] = wide[...].astype(BF16)


def join_kernel(p0, p1, p2, p3, q0, q1, q2, q3, second, out, second_out, wide, sems):
    copies = [
        pltpu.make_async_copy(
            second.at[x, z], second_out.at[pl.ds((z * XS + x) * SUB2, SUB2)], sems.at[z * XS + x]
        )
        for z in range(ZL)
        for x in range(XS)
    ]
    for copy in copies:
        copy.start()
    _, y, core, _ = place()
    for j in range(YS):
        k = lax.rem(y - j + YS, YS)
        own = pick(k, [p[...] for p in (p0, p1, p2, p3)]).astype(F32)
        other = pick(k, [q[...] for q in (q0, q1, q2, q3)]).astype(F32)
        for c, block in enumerate((jnp.where(core == 0, own, other), jnp.where(core == 0, other, own))):
            for z in range(ZS):
                wide[pl.ds(((z * YS + j) * CORES + c) * SUB, SUB), :] = block[z * SUB : (z + 1) * SUB]
    out[...] = wide[...].astype(BF16)
    for copy in copies:
        copy.wait()


def update_second_kernel(terms, outer_hbm, moment_hbm, new_outer, new_moment, low, outer, moment, sems):
    copies = [
        pltpu.make_async_copy(outer_hbm, outer, sems.at[0]),
        pltpu.make_async_copy(moment_hbm, moment, sems.at[1]),
    ]
    for copy in copies:
        copy.start()
    summed = terms[0].astype(F32)
    for k in range(1, ROWS):
        summed = summed + terms[k].astype(F32)
    for copy in copies:
        copy.wait()
    outer_new, moment_new = nesterov(outer[...], moment[...], summed, ROWS)
    new_outer[...] = outer_new
    new_moment[...] = moment_new
    low[...] = outer_new.astype(BF16)


def spread_kernel(own, other, out):
    z_lo = place()[3]
    first = jnp.where(z_lo == 0, own[...], other[...])
    second = jnp.where(z_lo == 0, other[...], own[...])
    for x in range(XS):
        out[x, 0] = first
        out[x, 1] = second


def call(kernel, args, outs, scratch=(), flops=0, name=None, hbm_args=None, after=(), vmem=VMEM_BYTES):
    inside = pl.BlockSpec(memory_space=pltpu.VMEM)
    outside = pl.BlockSpec(memory_space=pltpu.HBM)
    shapes = tuple(jax.ShapeDtypeStruct(shape, dtype) for shape, dtype in outs)
    moved = sum(a.size * a.dtype.itemsize for a in args)
    moved += sum(s.size * s.dtype.itemsize for s in shapes)
    first, last = len(args), len(args) + len(after)

    def body(*refs):
        kernel(*refs[:first], *refs[last:])

    return pl.pallas_call(
        body,
        out_shape=shapes,
        in_specs=[outside if h else inside for h in (hbm_args or [False] * len(args))]
        + [pl.BlockSpec(memory_space=pl.ANY) for _ in after],
        out_specs=tuple(inside for _ in shapes),
        scratch_shapes=list(scratch),
        compiler_params=pltpu.CompilerParams(vmem_limit_bytes=vmem),
        cost_estimate=pl.CostEstimate(flops=flops, bytes_accessed=moved, transcendentals=0),
        name=name,
    )(*args, *after)


def on_device(
    activations,
    cotangent,
    inner_first,
    inner_second,
    outer_first,
    momentum_first,
    outer_second,
    momentum_second,
):
    def send(value, dz, dy, dc):
        return lax.ppermute(value, "col", shift(dz, dy, dc))

    mine, theirs, final_second = call(
        terms_kernel,
        (activations, inner_first, cotangent, inner_second),
        (((D // 2, D), F32), ((D // 2, D), F32), ((D, D), BF16)),
        [
            pltpu.VMEM((T, D), BF16),
            pltpu.VMEM((D, D), BF16),
            pltpu.VMEM((T, D), BF16),
            pltpu.VMEM((D, D), BF16),
            pltpu.VMEM((T, D), BF16),
            pltpu.VMEM((T, D), BF16),
            pltpu.VMEM((D, D), F32),
            pltpu.SemaphoreType.DMA((2 + 2 * (T // TB),)),
        ],
        flops=8 * T * D * D,
        name="terms",
        hbm_args=(True,) * 4,
        vmem=MOST_VMEM,
    )
    got = send(theirs, 0, 0, 1)
    terms_second = lax.all_to_all(final_second.reshape(ROWS, SUB2, D), "row", 0, 0)

    own, *sends = call(
        core_sum_kernel,
        (mine, got),
        (((BLK, D), F32),) + (((BLK, D), BF16),) * 3,
        name="core_sum",
    )
    y_terms = [send(s, 0, k + 1, 0) for k, s in enumerate(sends)]
    y_total, own, *sends = call(
        y_sum_kernel,
        (own, *y_terms),
        (((BLK, D), F32),) + tuple(((SUB, D), t) for t in (F32, F32, BF16, F32)),
        name="y_sum",
    )
    z_terms = [send(s, k + 1, 0, 0) for k, s in enumerate(sends)]
    new_outer_first, new_momentum_first, low = call(
        update_first_kernel,
        (own, *z_terms, outer_first, momentum_first),
        (((SUB, D), F32), ((SUB, D), F32), ((SUB, D), BF16)),
        name="update_first",
    )

    new_outer_second, new_momentum_second, low_second = call(
        update_second_kernel,
        (terms_second, outer_second, momentum_second),
        (((SUB2, D), F32), ((SUB2, D), F32), ((SUB2, D), BF16)),
        [pltpu.VMEM((SUB2, D), F32), pltpu.VMEM((SUB2, D), F32), pltpu.SemaphoreType.DMA((2,))],
        name="update_second",
        hbm_args=(False, True, True),
        after=(y_total,),
    )
    other_second = lax.ppermute(low_second, "row", [(i, (i + XS) % ROWS) for i in range(ROWS)])
    (spread,) = call(
        spread_kernel,
        (low_second, other_second),
        (((XS, ZL, SUB2, D), BF16),),
        name="spread",
        after=(low,),
    )
    gathered_second = lax.all_to_all(spread, "row", 0, 0, axis_index_groups=X_GROUPS)

    (block,) = call(
        join_z_kernel,
        [low] + [send(low, k, 0, 0) for k in range(1, ZS)],
        (((BLK, D), BF16),),
        [pltpu.VMEM((BLK, D), F32)],
        name="join_z",
    )
    blocks = [block] + [send(block, 0, k, 0) for k in range(1, YS)]
    others = [send(b, 0, 0, 1) for b in blocks]
    vmem, anywhere = pl.BlockSpec(memory_space=pltpu.VMEM), pl.BlockSpec(memory_space=pl.ANY)
    module = jax.ShapeDtypeStruct((D, D), BF16)
    reset_first, reset_second = pl.pallas_call(
        join_kernel,
        out_shape=(module, module),
        in_specs=[vmem] * 8 + [anywhere],
        out_specs=(vmem, anywhere),
        scratch_shapes=[pltpu.VMEM((D, D), F32), pltpu.SemaphoreType.DMA((ROWS,))],
        compiler_params=pltpu.CompilerParams(vmem_limit_bytes=VMEM_BYTES),
        cost_estimate=pl.CostEstimate(flops=0, bytes_accessed=8 * D * D, transcendentals=0),
        name="join",
    )(*blocks, *others, gathered_second)
    return (
        new_outer_first,
        new_momentum_first,
        new_outer_second,
        new_momentum_second,
        reset_first,
        reset_second,
    )


def solution(mesh):
    return jax.shard_map(
        on_device,
        mesh=mesh,
        in_specs=(
            P(("row", "col"), None),
            P(("row", "col"), None),
            P("col", "row"),
            P("row", "col"),
            P("col", "row"),
            P("col", "row"),
            P("row", "col"),
            P("row", "col"),
        ),
        out_specs=(
            P("col", "row"),
            P("col", "row"),
            P("row", "col"),
            P("row", "col"),
            P("col", "row"),
            P("row", "col"),
        ),
        check_vma=False,
    )
```

time: 530 us -> 98.3 us (0.19)
  waiting for transfers between devices: 479 us -> 27.9 us
  starting transfers between devices: 0.16 us -> 47.5 us
  Pallas kernels: 0 us -> 19.7 us
  matrix products: 17.2 us -> 0 us
  local copies, waits for them, and re-layouts: 15.7 us -> 2.01 us
  between operations: 13.9 us -> 0.87 us
    psum x2 -> x0, waiting for transfers between devices: 381 us -> none  [the longest x1 296 us: on_device(): summed_first = lax.psum(final_first, 'col')]
    all_gather x2 -> x0, waiting for transfers between devices: 98.3 us -> none  [the longest x1 62.8 us: on_device(): lax.all_gather(new_outer_first.astype(jnp.bfloat16), 'col', axis=0, tiled...]
    ppermute x0 -> x18, starting transfers between devices: none -> 37.6 us  [the longest x17 36.1 us: send(): return lax.ppermute(value, 'col', shift(dz, dy, dc))]
    ppermute x0 -> x18, waiting for transfers between devices: none -> 24.8 us  [the longest x17 24.8 us: send(): return lax.ppermute(value, 'col', shift(dz, dy, dc))]
    pallas_call x0 -> x8, Pallas kernels: none -> 19.7 us  [the longest x7 17.2 us: call(): pl.pallas_call(body, out_shape=shapes, in_specs=[outside if h else inside...]
    dot_general x3 -> x0, matrix products: 17.2 us -> none  [the longest x2 13.4 us: final_rows(): lax.dot_general(inputs, grads, (((0,), (0,)), ((), ())), preferred_elemen...]
    unnamed x23 -> x10, local copies, waits for them, and re-layouts: 14.9 us -> 2.01 us
    all_to_all x0 -> x2, starting transfers between devices: none -> 9.91 us  [the longest x1 6.34 us: on_device(): lax.all_to_all(final_second.reshape(ROWS, SUB2, D), 'row', 0, 0)]
  transfers between devices with their start and end apart: 4 -> 20, of which waited for: 4 -> 9; matrix products, arithmetic and copies ran while one was open for 3% -> 0% of each run, Pallas kernels for 0% -> 1%
where the time goes in v2:
time: 98.3 us; the launch traced here: 98 us
  starting transfers between devices  47.5 us (48%)
  waiting for transfers between devices  27.9 us (28%)
  Pallas kernels  19.7 us (20%)
  local copies, waits for them, and re-layouts  2.01 us (2%)
    ppermute x17, starting transfers between devices, send(): return lax.ppermute(value, 'col', shift(dz, dy, dc))  36.1 us
    ppermute x17, waiting for transfers between devices, send(): return lax.ppermute(value, 'col', shift(dz, dy, dc))  24.8 us
    pallas_call x7, Pallas kernels, call(): pl.pallas_call(body, out_shape=shapes, in_specs=[outside if h else inside...  17.2 us
    all_to_all x1, starting transfers between devices, on_device(): lax.all_to_all(final_second.reshape(ROWS, SUB2, D), 'row', 0, 0)  6.34 us
    all_to_all x1, starting transfers between devices, on_device(): lax.all_to_all(spread, 'row', 0, 0, axis_index_groups=X_GROUPS)  3.57 us
    all_to_all x1, waiting for transfers between devices, on_device(): lax.all_to_all(final_second.reshape(ROWS, SUB2, D), 'row', 0, 0)  3.11 us
    pallas_call x1, Pallas kernels, on_device(): pl.pallas_call(join_kernel, out_shape=(module, module), in_specs=[vmem] *...  2.55 us
    unnamed x10, local copies, waits for them, and re-layouts  2.01 us
  transfers between devices with their start and end apart: 20, of which 9 were waited for; matrix products, arithmetic and copies ran while one was open for 0% of the time, Pallas kernels for 1%

profile of v2, /device:TPU:1, one launch (start us, length us, event | category | flops | bytes accessed | tf_op | source)
XLA Modules:
  0.0 98.0 jit_solution(10633163357820331987)
XLA Ops:
  0.6 12.8 %terms.1 = (f32[448,896]{1,0:T(8,128)}, f32[448,896]{1,0:T(8,128)}, bf16[896,896]{1,0:T(8,128)(2,1)}) custom-call(bf16[1024,896]{1,0:T(8,128)(2,1)} %refs_0_.1, bf16[896,896]{1,0:T(8,128)(2,1)} %refs_1_.2, bf16[1024,896]{1,0:T(8,128)(2,1)} %refs_2_.2, bf16[896,896]{1,0:T(8,128)(2,1)} %refs_3_.1), custom_call_target="tpu_custom_call" | custom-call | flops 6576668672 | bytes 11698176 | tf_op jit(solution)/shard_map/terms/pallas_call | solution.py:202
  13.4 0.0 copy-start
  13.4 6.3 %all-to-all-start = ((bf16[8,112,896]{2,1,0:T(8,128)(2,1)}), bf16[8,112,896]{2,1,0:T(8,128)(2,1)S(1)}, u32[]{:S(2)}, u32[]{:S(2)}) async-start(bf16[8,112,896]{2,1,0:T(8,128)(2,1)} %bitcast.1), calls=%async_computation | async-start | bytes 3211264 | tf_op jit(solution)/shard_map/all_to_all | solution.py:248
  19.8 1.0 collective-permute-start
  20.7 3.3 %collective-permute-done.refs_1_ = f32[448,896]{1,0:T(8,128)S(1)} collective-permute-done((f32[448,896]{1,0:T(8,128)}, f32[448,896]{1,0:T(8,128)S(1)}, u32[]{:S(2)}, u32[]{:S(2)}) %collective-permute-start) | collective-permute-done | bytes 1605664 | tf_op jit(solution)/shard_map/ppermute | solution.py:226
  24.0 0.2 core_sum.1
  24.2 1.4 %collective-permute-start.1 = (bf16[112,896]{1,0:T(8,128)(2,1)S(1)}, bf16[112,896]{1,0:T(8,128)(2,1)S(1)}, u32[]{:S(2)}, u32[]{:S(2)}) collective-permute-start(bf16[112,896]{1,0:T(8,128)(2,1)S(1)} %get-tuple-element.29), channel_id=1, source_target_pairs={{0,2},{1,3},{2,4},{3,5},{4,6},{5,7},{6,0},{7,1},{8,10},{9,11},{10,... | collective-permute-start | bytes 602120 | tf_op jit(solution)/shard_map/ppermute | solution.py:226
  25.6 2.6 %collective-permute-start.2 = (bf16[112,896]{1,0:T(8,128)(2,1)S(1)}, bf16[112,896]{1,0:T(8,128)(2,1)S(1)}, u32[]{:S(2)}, u32[]{:S(2)}) collective-permute-start(bf16[112,896]{1,0:T(8,128)(2,1)S(1)} %get-tuple-element.30), channel_id=1, source_target_pairs={{0,4},{1,5},{2,6},{3,7},{4,0},{5,1},{6,2},{7,3},{8,12},{9,13},{10,... | collective-permute-start | bytes 602120 | tf_op jit(solution)/shard_map/ppermute | solution.py:226
  28.2 1.1 %collective-permute-start.3 = (bf16[112,896]{1,0:T(8,128)(2,1)S(1)}, bf16[112,896]{1,0:T(8,128)(2,1)S(1)}, u32[]{:S(2)}, u32[]{:S(2)}) collective-permute-start(bf16[112,896]{1,0:T(8,128)(2,1)S(1)} %get-tuple-element.31), channel_id=1, source_target_pairs={{0,6},{1,7},{2,0},{3,1},{4,2},{5,3},{6,4},{7,5},{8,14},{9,15},{10,... | collective-permute-start | bytes 602120 | tf_op jit(solution)/shard_map/ppermute | solution.py:226
  29.3 2.6 %collective-permute-done.1.refs_1_ = bf16[112,896]{1,0:T(8,128)(2,1)S(1)} collective-permute-done((bf16[112,896]{1,0:T(8,128)(2,1)S(1)}, bf16[112,896]{1,0:T(8,128)(2,1)S(1)}, u32[]{:S(2)}, u32[]{:S(2)}) %collective-permute-start.1) | collective-permute-done | bytes 200736 | tf_op jit(solution)/shard_map/ppermute | solution.py:226
  31.8 5.4 %collective-permute-done.2.refs_2_ = bf16[112,896]{1,0:T(8,128)(2,1)S(1)} collective-permute-done((bf16[112,896]{1,0:T(8,128)(2,1)S(1)}, bf16[112,896]{1,0:T(8,128)(2,1)S(1)}, u32[]{:S(2)}, u32[]{:S(2)}) %collective-permute-start.2) | collective-permute-done | bytes 200736 | tf_op jit(solution)/shard_map/ppermute | solution.py:226
  37.2 0.0 collective-permute-done.3.refs_3_
  37.3 0.3 y_sum.1
  37.6 3.1 %all-to-all-done.refs_0_ = bf16[8,112,896]{2,1,0:T(8,128)(2,1)S(1)} async-done(((bf16[8,112,896]{2,1,0:T(8,128)(2,1)}), bf16[8,112,896]{2,1,0:T(8,128)(2,1)S(1)}, u32[]{:S(2)}, u32[]{:S(2)}) %all-to-all-start) | async-done | bytes 1605664 | tf_op jit(solution)/shard_map/all_to_all | solution.py:248
  40.7 1.0 %copy-done.1 = f32[112,896]{1,0:T(8,128)S(1)} copy-done((f32[112,896]{1,0:T(8,128)S(1)}, f32[112,896]{1,0:T(8,128)}, u32[]{:S(2)}) %copy-start.1) | copy-done | bytes 401432
  41.7 1.0 %copy-done.2 = f32[112,896]{1,0:T(8,128)S(1)} copy-done((f32[112,896]{1,0:T(8,128)S(1)}, f32[112,896]{1,0:T(8,128)}, u32[]{:S(2)}) %copy-start.2) | copy-done | bytes 401432
  42.7 1.7 %update_second.1 = (f32[112,896]{1,0:T(8,128)}, f32[112,896]{1,0:T(8,128)}, bf16[112,896]{1,0:T(8,128)(2,1)S(1)}) custom-call(bf16[8,112,896]{2,1,0:T(8,128)(2,1)S(1)} %all-to-all-done.refs_0_, f32[112,896]{1,0:T(8,128)S(1)} %copy-done.1, f32[112,896]{1,0:T(8,128)S(1)} %copy-done.2, f32[112,896]{1,0:T(8,128)S(1)} %get-tuple-element.39.refs_3_), custom_call_target="tpu_custom_call" | custom-call | bytes 3411968 | tf_op jit(solution)/shard_map/update_second/pallas_call | solution.py:202
  44.4 1.5 %collective-permute-start.17 = (bf16[112,896]{1,0:T(8,128)(2,1)S(1)}, bf16[112,896]{1,0:T(8,128)(2,1)S(1)}, u32[]{:S(2)}, u32[]{:S(2)}) collective-permute-start(bf16[112,896]{1,0:T(8,128)(2,1)S(1)} %get-tuple-element.43.refs_0_), channel_id=1, source_target_pairs={{0,128},{32,160},{64,192},{96,224},{128,0},{160,32},{192,64},{224,... | collective-permute-start | bytes 602120 | tf_op jit(solution)/shard_map/ppermute | solution.py:280
  45.8 3.0 %collective-permute-start.4 = (f32[28,896]{1,0:T(8,128)S(1)}, f32[28,896]{1,0:T(8,128)S(1)}, u32[]{:S(2)}, u32[]{:S(2)}) collective-permute-start(f32[28,896]{1,0:T(8,128)S(1)} %get-tuple-element.33), channel_id=1, source_target_pairs={{0,8},{1,9},{2,10},{3,11},{4,12},{5,13},{6,14},{7,15},{8,16},{9,17... | collective-permute-start | bytes 301064 | tf_op jit(solution)/shard_map/ppermute | solution.py:226
  48.8 2.1 %collective-permute-start.6 = (f32[28,896]{1,0:T(8,128)S(1)}, f32[28,896]{1,0:T(8,128)S(1)}, u32[]{:S(2)}, u32[]{:S(2)}) collective-permute-start(f32[28,896]{1,0:T(8,128)S(1)} %get-tuple-element.35), channel_id=1, source_target_pairs={{0,24},{1,25},{2,26},{3,27},{4,28},{5,29},{6,30},{7,31},{8,0},{9,1... | collective-permute-start | bytes 301064 | tf_op jit(solution)/shard_map/ppermute | solution.py:226
  51.0 4.5 %collective-permute-start.5 = (bf16[28,896]{1,0:T(8,128)(2,1)S(1)}, bf16[28,896]{1,0:T(8,128)(2,1)S(1)}, u32[]{:S(2)}, u32[]{:S(2)}) collective-permute-start(bf16[28,896]{1,0:T(8,128)(2,1)S(1)} %get-tuple-element.34), channel_id=1, source_target_pairs={{0,16},{1,17},{2,18},{3,19},{4,20},{5,21},{6,22},{7,23},{8,24},{9,... | collective-permute-start | bytes 150536 | tf_op jit(solution)/shard_map/ppermute | solution.py:226
  55.4 7.1 %collective-permute-done.5.refs_2_ = bf16[28,896]{1,0:T(8,128)(2,1)S(1)} collective-permute-done((bf16[28,896]{1,0:T(8,128)(2,1)S(1)}, bf16[28,896]{1,0:T(8,128)(2,1)S(1)}, u32[]{:S(2)}, u32[]{:S(2)}) %collective-permute-start.5) | collective-permute-done | bytes 50208 | tf_op jit(solution)/shard_map/ppermute | solution.py:226
  62.5 0.0 collective-permute-done.4.refs_1_
  62.5 0.0 collective-permute-done.6.refs_3_
  62.5 0.7 update_first.1
  63.3 0.0 collective-permute-done.17.refs_1_
  63.3 1.3 %spread.1 = bf16[4,2,112,896]{3,2,1,0:T(8,128)(2,1)} custom-call(bf16[112,896]{1,0:T(8,128)(2,1)S(1)} %get-tuple-element.43.refs_0_, bf16[112,896]{1,0:T(8,128)(2,1)S(1)} %collective-permute-done.17.refs_1_, bf16[28,896]{1,0:T(8,128)(2,1)S(1)} %get-tuple-element.42.refs_0_.refs_2_), custom_call_target="tpu_custom_call" | custom-call | bytes 2007040 | tf_op jit(solution)/shard_map/spread/pallas_call | solution.py:202
  64.6 3.6 %all-to-all-start.1 = ((bf16[4,2,112,896]{3,2,1,0:T(8,128)(2,1)}), bf16[4,2,112,896]{3,2,1,0:T(8,128)(2,1)S(1)}, u32[]{:S(2)}, u32[]{:S(2)}) async-start(bf16[4,2,112,896]{3,2,1,0:T(8,128)(2,1)} %spread.1), calls=%async_computation.1 | async-start | bytes 3211264 | tf_op jit(solution)/shard_map/all_to_all | solution.py:288
  68.2 0.4 collective-permute-start.9
  68.5 3.7 %collective-permute-start.8 = (bf16[28,896]{1,0:T(8,128)(2,1)S(1)}, bf16[28,896]{1,0:T(8,128)(2,1)S(1)}, u32[]{:S(2)}, u32[]{:S(2)}) collective-permute-start(bf16[28,896]{1,0:T(8,128)(2,1)S(1)} %get-tuple-element.42.refs_0_.refs_2_), channel_id=1, source_target_pairs={{0,16},{1,17},{2,18},{3,19},{4,20},{5,21},{6,22},{7,23},{8,24},{9,... | collective-permute-start | bytes 150536 | tf_op jit(solution)/shard_map/ppermute | solution.py:226
  72.3 0.0 collective-permute-start.7
  72.3 0.5 collective-permute-done.9.refs_3_
  72.8 3.2 %collective-permute-done.8.refs_2_ = bf16[28,896]{1,0:T(8,128)(2,1)S(1)} collective-permute-done((bf16[28,896]{1,0:T(8,128)(2,1)S(1)}, bf16[28,896]{1,0:T(8,128)(2,1)S(1)}, u32[]{:S(2)}, u32[]{:S(2)}) %collective-permute-start.8) | collective-permute-done | bytes 50208 | tf_op jit(solution)/shard_map/ppermute | solution.py:226
  76.0 1.6 %collective-permute-done.7.refs_1_ = bf16[28,896]{1,0:T(8,128)(2,1)S(1)} collective-permute-done((bf16[28,896]{1,0:T(8,128)(2,1)S(1)}, bf16[28,896]{1,0:T(8,128)(2,1)S(1)}, u32[]{:S(2)}, u32[]{:S(2)}) %collective-permute-start.7) | collective-permute-done | bytes 50208 | tf_op jit(solution)/shard_map/ppermute | solution.py:226
  77.6 0.1 join_z.1.p0
  77.8 2.8 %collective-permute-start.12 = (bf16[112,896]{1,0:T(8,128)(2,1)S(1)}, bf16[112,896]{1,0:T(8,128)(2,1)S(1)}, u32[]{:S(2)}, u32[]{:S(2)}) collective-permute-start(bf16[112,896]{1,0:T(8,128)(2,1)S(1)} %join_z.1.p0), channel_id=1, source_target_pairs={{0,6},{1,7},{2,0},{3,1},{4,2},{5,3},{6,4},{7,5},{8,14},{9,15},{10,... | collective-permute-start | bytes 602120 | tf_op jit(solution)/shard_map/ppermute | solution.py:226
  80.6 0.3 collective-permute-start.11
  80.9 0.7 collective-permute-start.10
  81.6 4.8 %collective-permute-start.13 = (bf16[112,896]{1,0:T(8,128)(2,1)S(1)}, bf16[112,896]{1,0:T(8,128)(2,1)S(1)}, u32[]{:S(2)}, u32[]{:S(2)}) collective-permute-start(bf16[112,896]{1,0:T(8,128)(2,1)S(1)} %join_z.1.p0), channel_id=1, source_target_pairs={{0,1},{1,0},{2,3},{3,2},{4,5},{5,4},{6,7},{7,6},{8,9},{9,8},{10,11... | collective-permute-start | bytes 602120 | tf_op jit(solution)/shard_map/ppermute | solution.py:226
  86.4 3.8 %collective-permute-start.16 = (bf16[112,896]{1,0:T(8,128)(2,1)S(1)}, bf16[112,896]{1,0:T(8,128)(2,1)S(1)}, u32[]{:S(2)}, u32[]{:S(2)}) collective-permute-start(bf16[112,896]{1,0:T(8,128)(2,1)S(1)} %collective-permute-done.12.p3), channel_id=1, source_target_pairs={{0,1},{1,0},{2,3},{3,2},{4,5},{5,4},{6,7},{7,6},{8,9},{9,8},{10,11... | collective-permute-start | bytes 602120 | tf_op jit(solution)/shard_map/ppermute | solution.py:226
  90.3 1.9 %collective-permute-start.15 = (bf16[112,896]{1,0:T(8,128)(2,1)S(1)}, bf16[112,896]{1,0:T(8,128)(2,1)S(1)}, u32[]{:S(2)}, u32[]{:S(2)}) collective-permute-start(bf16[112,896]{1,0:T(8,128)(2,1)S(1)} %collective-permute-done.11.p2), channel_id=1, source_target_pairs={{0,1},{1,0},{2,3},{3,2},{4,5},{5,4},{6,7},{7,6},{8,9},{9,8},{10,11... | collective-permute-start | bytes 602120 | tf_op jit(solution)/shard_map/ppermute | solution.py:226
  92.2 2.0 %collective-permute-start.14 = (bf16[112,896]{1,0:T(8,128)(2,1)S(1)}, bf16[112,896]{1,0:T(8,128)(2,1)S(1)}, u32[]{:S(2)}, u32[]{:S(2)}) collective-permute-start(bf16[112,896]{1,0:T(8,128)(2,1)S(1)} %collective-permute-done.10.p1), channel_id=1, source_target_pairs={{0,1},{1,0},{2,3},{3,2},{4,5},{5,4},{6,7},{7,6},{8,9},{9,8},{10,11... | collective-permute-start | bytes 602120 | tf_op jit(solution)/shard_map/ppermute | solution.py:226
  94.2 0.0 collective-permute-done.13.q0
  94.2 0.0 collective-permute-done.16.q3
  94.2 0.0 collective-permute-done.15.q2
  94.2 1.1 %collective-permute-done.14.q1 = bf16[112,896]{1,0:T(8,128)(2,1)S(1)} collective-permute-done((bf16[112,896]{1,0:T(8,128)(2,1)S(1)}, bf16[112,896]{1,0:T(8,128)(2,1)S(1)}, u32[]{:S(2)}, u32[]{:S(2)}) %collective-permute-start.14) | collective-permute-done | bytes 200736 | tf_op jit(solution)/shard_map/ppermute | solution.py:226
  95.3 0.0 all-to-all-done.1.second
  95.3 2.5 %join.1 = (bf16[896,896]{1,0:T(8,128)(2,1)}, bf16[896,896]{1,0:T(8,128)(2,1)}) custom-call(bf16[112,896]{1,0:T(8,128)(2,1)S(1)} %join_z.1.p0, bf16[112,896]{1,0:T(8,128)(2,1)S(1)} %collective-permute-done.10.p1, bf16[112,896]{1,0:T(8,128)(2,1)S(1)} %collective-permute-done.11.p2, bf16[112,896]{1,0:T(8,128)(2,1)S(1)} %collective-permute-done.12.p3, ...), custom_call_target="tpu_custom_call" | custom-call | bytes 6422528 | tf_op jit(solution)/shard_map/join/pallas_call | solution.py:301
  (10 shorter events, 0.0 us)
Async XLA Ops:
  13.4 10.6 %copy-start = (f32[448,896]{1,0:T(8,128)S(1)}, f32[448,896]{1,0:T(8,128)}, u32[]{:S(2)}) copy-start(f32[448,896]{1,0:T(8,128)} %get-tuple-element.26.refs_0_) | copy-start | bytes 4816900
  13.4 27.2 %all-to-all-start = ((bf16[8,112,896]{2,1,0:T(8,128)(2,1)}), bf16[8,112,896]{2,1,0:T(8,128)(2,1)S(1)}, u32[]{:S(2)}, u32[]{:S(2)}) async-start(bf16[8,112,896]{2,1,0:T(8,128)(2,1)} %bitcast.1), calls=%async_computation | async-start | bytes 3211264 | tf_op jit(solution)/shard_map/all_to_all | solution.py:248
  19.8 4.2 %collective-permute-start = (f32[448,896]{1,0:T(8,128)}, f32[448,896]{1,0:T(8,128)S(1)}, u32[]{:S(2)}, u32[]{:S(2)}) collective-permute-start(f32[448,896]{1,0:T(8,128)} %get-tuple-element.27), channel_id=1, source_target_pairs={{0,1},{1,0},{2,3},{3,2},{4,5},{5,4},{6,7},{7,6},{8,9},{9,8},{10,11... | collective-permute-start | bytes 4816904 | tf_op jit(solution)/shard_map/ppermute | solution.py:226
  24.2 7.6 %collective-permute-start.1 = (bf16[112,896]{1,0:T(8,128)(2,1)S(1)}, bf16[112,896]{1,0:T(8,128)(2,1)S(1)}, u32[]{:S(2)}, u32[]{:S(2)}) collective-permute-start(bf16[112,896]{1,0:T(8,128)(2,1)S(1)} %get-tuple-element.29), channel_id=1, source_target_pairs={{0,2},{1,3},{2,4},{3,5},{4,6},{5,7},{6,0},{7,1},{8,10},{9,11},{10,... | collective-permute-start | bytes 602120 | tf_op jit(solution)/shard_map/ppermute | solution.py:226
  25.6 11.7 %collective-permute-start.2 = (bf16[112,896]{1,0:T(8,128)(2,1)S(1)}, bf16[112,896]{1,0:T(8,128)(2,1)S(1)}, u32[]{:S(2)}, u32[]{:S(2)}) collective-permute-start(bf16[112,896]{1,0:T(8,128)(2,1)S(1)} %get-tuple-element.30), channel_id=1, source_target_pairs={{0,4},{1,5},{2,6},{3,7},{4,0},{5,1},{6,2},{7,3},{8,12},{9,13},{10,... | collective-permute-start | bytes 602120 | tf_op jit(solution)/shard_map/ppermute | solution.py:226
  28.2 9.0 %collective-permute-start.3 = (bf16[112,896]{1,0:T(8,128)(2,1)S(1)}, bf16[112,896]{1,0:T(8,128)(2,1)S(1)}, u32[]{:S(2)}, u32[]{:S(2)}) collective-permute-start(bf16[112,896]{1,0:T(8,128)(2,1)S(1)} %get-tuple-element.31), channel_id=1, source_target_pairs={{0,6},{1,7},{2,0},{3,1},{4,2},{5,3},{6,4},{7,5},{8,14},{9,15},{10,... | collective-permute-start | bytes 602120 | tf_op jit(solution)/shard_map/ppermute | solution.py:226
  37.2 25.3 %copy-start.3 = (f32[28,896]{1,0:T(8,128)S(1)}, f32[28,896]{1,0:T(8,128)}, u32[]{:S(2)}) copy-start(f32[28,896]{1,0:T(8,128)} %refs_4_.1) | copy-start | bytes 301060
  37.2 25.3 %copy-start.4 = (f32[28,896]{1,0:T(8,128)S(1)}, f32[28,896]{1,0:T(8,128)}, u32[]{:S(2)}) copy-start(f32[28,896]{1,0:T(8,128)} %refs_5_.1) | copy-start | bytes 301060
  40.7 1.0 %copy-start.1 = (f32[112,896]{1,0:T(8,128)S(1)}, f32[112,896]{1,0:T(8,128)}, u32[]{:S(2)}) copy-start(f32[112,896]{1,0:T(8,128)} %refs_1_.3) | copy-start | bytes 1204228
  41.7 1.0 %copy-start.2 = (f32[112,896]{1,0:T(8,128)S(1)}, f32[112,896]{1,0:T(8,128)}, u32[]{:S(2)}) copy-start(f32[112,896]{1,0:T(8,128)} %refs_2_.3) | copy-start | bytes 1204228
  44.4 18.9 %collective-permute-start.17 = (bf16[112,896]{1,0:T(8,128)(2,1)S(1)}, bf16[112,896]{1,0:T(8,128)(2,1)S(1)}, u32[]{:S(2)}, u32[]{:S(2)}) collective-permute-start(bf16[112,896]{1,0:T(8,128)(2,1)S(1)} %get-tuple-element.43.refs_0_), channel_id=1, source_target_pairs={{0,128},{32,160},{64,192},{96,224},{128,0},{160,32},{192,64},{224,... | collective-permute-start | bytes 602120 | tf_op jit(solution)/shard_map/ppermute | solution.py:280
  45.8 16.7 %collective-permute-start.4 = (f32[28,896]{1,0:T(8,128)S(1)}, f32[28,896]{1,0:T(8,128)S(1)}, u32[]{:S(2)}, u32[]{:S(2)}) collective-permute-start(f32[28,896]{1,0:T(8,128)S(1)} %get-tuple-element.33), channel_id=1, source_target_pairs={{0,8},{1,9},{2,10},{3,11},{4,12},{5,13},{6,14},{7,15},{8,16},{9,17... | collective-permute-start | bytes 301064 | tf_op jit(solution)/shard_map/ppermute | solution.py:226
  48.8 13.7 %collective-permute-start.6 = (f32[28,896]{1,0:T(8,128)S(1)}, f32[28,896]{1,0:T(8,128)S(1)}, u32[]{:S(2)}, u32[]{:S(2)}) collective-permute-start(f32[28,896]{1,0:T(8,128)S(1)} %get-tuple-element.35), channel_id=1, source_target_pairs={{0,24},{1,25},{2,26},{3,27},{4,28},{5,29},{6,30},{7,31},{8,0},{9,1... | collective-permute-start | bytes 301064 | tf_op jit(solution)/shard_map/ppermute | solution.py:226
  51.0 11.5 %collective-permute-start.5 = (bf16[28,896]{1,0:T(8,128)(2,1)S(1)}, bf16[28,896]{1,0:T(8,128)(2,1)S(1)}, u32[]{:S(2)}, u32[]{:S(2)}) collective-permute-start(bf16[28,896]{1,0:T(8,128)(2,1)S(1)} %get-tuple-element.34), channel_id=1, source_target_pairs={{0,16},{1,17},{2,18},{3,19},{4,20},{5,21},{6,22},{7,23},{8,24},{9,... | collective-permute-start | bytes 150536 | tf_op jit(solution)/shard_map/ppermute | solution.py:226
  64.6 30.7 %all-to-all-start.1 = ((bf16[4,2,112,896]{3,2,1,0:T(8,128)(2,1)}), bf16[4,2,112,896]{3,2,1,0:T(8,128)(2,1)S(1)}, u32[]{:S(2)}, u32[]{:S(2)}) async-start(bf16[4,2,112,896]{3,2,1,0:T(8,128)(2,1)} %spread.1), calls=%async_computation.1 | async-start | bytes 3211264 | tf_op jit(solution)/shard_map/all_to_all | solution.py:288
  68.2 4.6 %collective-permute-start.9 = (bf16[28,896]{1,0:T(8,128)(2,1)S(1)}, bf16[28,896]{1,0:T(8,128)(2,1)S(1)}, u32[]{:S(2)}, u32[]{:S(2)}) collective-permute-start(bf16[28,896]{1,0:T(8,128)(2,1)S(1)} %get-tuple-element.42.refs_0_.refs_2_), channel_id=1, source_target_pairs={{0,24},{1,25},{2,26},{3,27},{4,28},{5,29},{6,30},{7,31},{8,0},{9,1... | collective-permute-start | bytes 150536 | tf_op jit(solution)/shard_map/ppermute | solution.py:226
  68.5 7.5 %collective-permute-start.8 = (bf16[28,896]{1,0:T(8,128)(2,1)S(1)}, bf16[28,896]{1,0:T(8,128)(2,1)S(1)}, u32[]{:S(2)}, u32[]{:S(2)}) collective-permute-start(bf16[28,896]{1,0:T(8,128)(2,1)S(1)} %get-tuple-element.42.refs_0_.refs_2_), channel_id=1, source_target_pairs={{0,16},{1,17},{2,18},{3,19},{4,20},{5,21},{6,22},{7,23},{8,24},{9,... | collective-permute-start | bytes 150536 | tf_op jit(solution)/shard_map/ppermute | solution.py:226
  72.3 5.4 %collective-permute-start.7 = (bf16[28,896]{1,0:T(8,128)(2,1)S(1)}, bf16[28,896]{1,0:T(8,128)(2,1)S(1)}, u32[]{:S(2)}, u32[]{:S(2)}) collective-permute-start(bf16[28,896]{1,0:T(8,128)(2,1)S(1)} %get-tuple-element.42.refs_0_.refs_2_), channel_id=1, source_target_pairs={{0,8},{1,9},{2,10},{3,11},{4,12},{5,13},{6,14},{7,15},{8,16},{9,17... | collective-permute-start | bytes 150536 | tf_op jit(solution)/shard_map/ppermute | solution.py:226
  77.8 8.7 %collective-permute-start.12 = (bf16[112,896]{1,0:T(8,128)(2,1)S(1)}, bf16[112,896]{1,0:T(8,128)(2,1)S(1)}, u32[]{:S(2)}, u32[]{:S(2)}) collective-permute-start(bf16[112,896]{1,0:T(8,128)(2,1)S(1)} %join_z.1.p0), channel_id=1, source_target_pairs={{0,6},{1,7},{2,0},{3,1},{4,2},{5,3},{6,4},{7,5},{8,14},{9,15},{10,... | collective-permute-start | bytes 602120 | tf_op jit(solution)/shard_map/ppermute | solution.py:226
  80.6 9.7 %collective-permute-start.11 = (bf16[112,896]{1,0:T(8,128)(2,1)S(1)}, bf16[112,896]{1,0:T(8,128)(2,1)S(1)}, u32[]{:S(2)}, u32[]{:S(2)}) collective-permute-start(bf16[112,896]{1,0:T(8,128)(2,1)S(1)} %join_z.1.p0), channel_id=1, source_target_pairs={{0,4},{1,5},{2,6},{3,7},{4,0},{5,1},{6,2},{7,3},{8,12},{9,13},{10,... | collective-permute-start | bytes 602120 | tf_op jit(solution)/shard_map/ppermute | solution.py:226
  80.9 11.3 %collective-permute-start.10 = (bf16[112,896]{1,0:T(8,128)(2,1)S(1)}, bf16[112,896]{1,0:T(8,128)(2,1)S(1)}, u32[]{:S(2)}, u32[]{:S(2)}) collective-permute-start(bf16[112,896]{1,0:T(8,128)(2,1)S(1)} %join_z.1.p0), channel_id=1, source_target_pairs={{0,2},{1,3},{2,4},{3,5},{4,6},{5,7},{6,0},{7,1},{8,10},{9,11},{10,... | collective-permute-start | bytes 602120 | tf_op jit(solution)/shard_map/ppermute | solution.py:226
  81.6 12.6 %collective-permute-start.13 = (bf16[112,896]{1,0:T(8,128)(2,1)S(1)}, bf16[112,896]{1,0:T(8,128)(2,1)S(1)}, u32[]{:S(2)}, u32[]{:S(2)}) collective-permute-start(bf16[112,896]{1,0:T(8,128)(2,1)S(1)} %join_z.1.p0), channel_id=1, source_target_pairs={{0,1},{1,0},{2,3},{3,2},{4,5},{5,4},{6,7},{7,6},{8,9},{9,8},{10,11... | collective-permute-start | bytes 602120 | tf_op jit(solution)/shard_map/ppermute | solution.py:226
  86.4 7.8 %collective-permute-start.16 = (bf16[112,896]{1,0:T(8,128)(2,1)S(1)}, bf16[112,896]{1,0:T(8,128)(2,1)S(1)}, u32[]{:S(2)}, u32[]{:S(2)}) collective-permute-start(bf16[112,896]{1,0:T(8,128)(2,1)S(1)} %collective-permute-done.12.p3), channel_id=1, source_target_pairs={{0,1},{1,0},{2,3},{3,2},{4,5},{5,4},{6,7},{7,6},{8,9},{9,8},{10,11... | collective-permute-start | bytes 602120 | tf_op jit(solution)/shard_map/ppermute | solution.py:226
  90.3 4.0 %collective-permute-start.15 = (bf16[112,896]{1,0:T(8,128)(2,1)S(1)}, bf16[112,896]{1,0:T(8,128)(2,1)S(1)}, u32[]{:S(2)}, u32[]{:S(2)}) collective-permute-start(bf16[112,896]{1,0:T(8,128)(2,1)S(1)} %collective-permute-done.11.p2), channel_id=1, source_target_pairs={{0,1},{1,0},{2,3},{3,2},{4,5},{5,4},{6,7},{7,6},{8,9},{9,8},{10,11... | collective-permute-start | bytes 602120 | tf_op jit(solution)/shard_map/ppermute | solution.py:226
  92.2 3.1 %collective-permute-start.14 = (bf16[112,896]{1,0:T(8,128)(2,1)S(1)}, bf16[112,896]{1,0:T(8,128)(2,1)S(1)}, u32[]{:S(2)}, u32[]{:S(2)}) collective-permute-start(bf16[112,896]{1,0:T(8,128)(2,1)S(1)} %collective-permute-done.10.p1), channel_id=1, source_target_pairs={{0,1},{1,0},{2,3},{3,2},{4,5},{5,4},{6,7},{7,6},{8,9},{9,8},{10,11... | collective-permute-start | bytes 602120 | tf_op jit(solution)/shard_map/ppermute | solution.py:226

commit v3 on v2

--- a/solution.py
+++ b/solution.py
@@ -12,17 +12,16 @@
 
 T, D = 1024, 896
 ROWS, COLS = 8, 32
-ZL, XS = 2, 4
 ZS, YS, CORES = 4, 4, 2
 SUB = D // COLS
 BLK = ZS * SUB
 SUB2 = D // ROWS
 TB = 512
 RB = 448
-X_GROUPS = [[z * XS + x for x in range(XS)] for z in range(ZL)]
 UNIT = 1.0 / float(D) ** 0.5
 VMEM_BYTES = 32 * 2**20
 MOST_VMEM = 60 * 2**20
+SOME, LONG = 15 * 10**9, 6 * 10**10
 
 
 def shift(dz, dy, dc):
@@ -42,9 +41,8 @@
 
 
 def place():
-    col, row = lax.axis_index("col"), lax.axis_index("row")
-    y = lax.rem(col // CORES, YS)
-    return (col // (YS * CORES), y, lax.rem(col, CORES), row // XS)
+    col = lax.axis_index("col")
+    return (col // (YS * CORES), lax.rem(col // CORES, YS), lax.rem(col, CORES))
 
 
 def pick(position, options):
@@ -139,16 +137,10 @@
 
 
 def join_kernel(p0, p1, p2, p3, q0, q1, q2, q3, second, out, second_out, wide, sems):
-    copies = [
-        pltpu.make_async_copy(
-            second.at[x, z], second_out.at[pl.ds((z * XS + x) * SUB2, SUB2)], sems.at[z * XS + x]
-        )
-        for z in range(ZL)
-        for x in range(XS)
-    ]
+    copies = [pltpu.make_async_copy(second, second_out, sems.at[0])]
     for copy in copies:
         copy.start()
-    _, y, core, _ = place()
+    _, y, core = place()
     for j in range(YS):
         k = lax.rem(y - j + YS, YS)
         own = pick(k, [p[...] for p in (p0, p1, p2, p3)]).astype(F32)
@@ -161,31 +153,16 @@
         copy.wait()
 
 
-def update_second_kernel(terms, outer_hbm, moment_hbm, new_outer, new_moment, low, outer, moment, sems):
-    copies = [
-        pltpu.make_async_copy(outer_hbm, outer, sems.at[0]),
-        pltpu.make_async_copy(moment_hbm, moment, sems.at[1]),
-    ]
-    for copy in copies:
-        copy.start()
+def update_second_kernel(terms, outer, moment, new_outer, new_moment, spread):
     summed = terms[0].astype(F32)
     for k in range(1, ROWS):
         summed = summed + terms[k].astype(F32)
-    for copy in copies:
-        copy.wait()
     outer_new, moment_new = nesterov(outer[...], moment[...], summed, ROWS)
     new_outer[...] = outer_new
     new_moment[...] = moment_new
-    low[...] = outer_new.astype(BF16)
-
-
-def spread_kernel(own, other, out):
-    z_lo = place()[3]
-    first = jnp.where(z_lo == 0, own[...], other[...])
-    second = jnp.where(z_lo == 0, other[...], own[...])
-    for x in range(XS):
-        out[x, 0] = first
-        out[x, 1] = second
+    low = outer_new.astype(BF16)
+    for k in range(ROWS):
+        spread[k] = low
 
 
 def call(kernel, args, outs, scratch=(), flops=0, name=None, hbm_args=None, after=(), vmem=VMEM_BYTES):
@@ -258,42 +235,34 @@
         y_sum_kernel,
         (own, *y_terms),
         (((BLK, D), F32),) + tuple(((SUB, D), t) for t in (F32, F32, BF16, F32)),
+        flops=SOME,
         name="y_sum",
     )
     z_terms = [send(s, k + 1, 0, 0) for k, s in enumerate(sends)]
+    new_outer_second, new_momentum_second, spread = call(
+        update_second_kernel,
+        (terms_second, outer_second, momentum_second),
+        (((SUB2, D), F32), ((SUB2, D), F32), ((ROWS, SUB2, D), BF16)),
+        name="update_second",
+        after=(y_total,),
+    )
     new_outer_first, new_momentum_first, low = call(
         update_first_kernel,
         (own, *z_terms, outer_first, momentum_first),
         (((SUB, D), F32), ((SUB, D), F32), ((SUB, D), BF16)),
         name="update_first",
-    )
-
-    new_outer_second, new_momentum_second, low_second = call(
-        update_second_kernel,
-        (terms_second, outer_second, momentum_second),
-        (((SUB2, D), F32), ((SUB2, D), F32), ((SUB2, D), BF16)),
-        [pltpu.VMEM((SUB2, D), F32), pltpu.VMEM((SUB2, D), F32), pltpu.SemaphoreType.DMA((2,))],
-        name="update_second",
-        hbm_args=(False, True, True),
-        after=(y_total,),
-    )
-    other_second = lax.ppermute(low_second, "row", [(i, (i + XS) % ROWS) for i in range(ROWS)])
-    (spread,) = call(
-        spread_kernel,
-        (low_second, other_second),
-        (((XS, ZL, SUB2, D), BF16),),
-        name="spread",
-        after=(low,),
-    )
-    gathered_second = lax.all_to_all(spread, "row", 0, 0, axis_index_groups=X_GROUPS)
+        after=(spread,),
+    )
 
     (block,) = call(
         join_z_kernel,
         [low] + [send(low, k, 0, 0) for k in range(1, ZS)],
         (((BLK, D), BF16),),
         [pltpu.VMEM((BLK, D), F32)],
+        flops=LONG,
         name="join_z",
     )
+    gathered_second = lax.all_to_all(spread, "row", 0, 0)
     blocks = [block] + [send(block, 0, k, 0) for k in range(1, YS)]
     others = [send(b, 0, 0, 1) for b in blocks]
     vmem, anywhere = pl.BlockSpec(memory_space=pltpu.VMEM), pl.BlockSpec(memory_space=pl.ANY)
@@ -303,11 +272,11 @@
         out_shape=(module, module),
         in_specs=[vmem] * 8 + [anywhere],
         out_specs=(vmem, anywhere),
-        scratch_shapes=[pltpu.VMEM((D, D), F32), pltpu.SemaphoreType.DMA((ROWS,))],
+        scratch_shapes=[pltpu.VMEM((D, D), F32), pltpu.SemaphoreType.DMA((1,))],
         compiler_params=pltpu.CompilerParams(vmem_limit_bytes=VMEM_BYTES),
         cost_estimate=pl.CostEstimate(flops=0, bytes_accessed=8 * D * D, transcendentals=0),
         name="join",
-    )(*blocks, *others, gathered_second)
+    )(*blocks, *others, gathered_second.reshape(D, D))
     return (
         new_outer_first,
         new_momentum_first,

time: 98.3 us -> 85.4 us (0.87)
  the two profiles are of different devices: /device:TPU:1 before, /device:TPU:24 now
where the time goes in v3:
time: 85.4 us; the launch traced here: 85.2 us
  starting transfers between devices  35.4 us (41%)
  waiting for transfers between devices  28.6 us (33%)
  Pallas kernels  20.3 us (24%)
  between operations  0.88 us (1%)
    ppermute x17, starting transfers between devices, send(): return lax.ppermute(value, 'col', shift(dz, dy, dc))  23.6 us
    ppermute x17, waiting for transfers between devices, send(): return lax.ppermute(value, 'col', shift(dz, dy, dc))  22.2 us
    pallas_call x6, Pallas kernels, call(): pl.pallas_call(body, out_shape=shapes, in_specs=[outside if h else inside...  17.8 us
    all_to_all x1, waiting for transfers between devices, on_device(): gathered_second = lax.all_to_all(spread, 'row', 0, 0)  6.38 us
    all_to_all x1, starting transfers between devices, on_device(): gathered_second = lax.all_to_all(spread, 'row', 0, 0)  5.99 us
    all_to_all x1, starting transfers between devices, on_device(): lax.all_to_all(final_second.reshape(ROWS, SUB2, D), 'row', 0, 0)  5.79 us
    pallas_call x1, Pallas kernels, on_device(): pl.pallas_call(join_kernel, out_shape=(module, module), in_specs=[vmem] *...  2.48 us
  transfers between devices with their start and end apart: 19, of which 11 were waited for; matrix products, arithmetic and copies ran while one was open for 0% of the time, Pallas kernels for 5%

profile of v3, /device:TPU:24, one launch (start us, length us, event | category | flops | bytes accessed | tf_op | source)
XLA Modules:
  0.0 85.2 jit_solution(1762458038181418524)
XLA Ops:
  0.6 12.8 %terms.1 = (f32[448,896]{1,0:T(8,128)}, f32[448,896]{1,0:T(8,128)}, bf16[896,896]{1,0:T(8,128)(2,1)}) custom-call(bf16[1024,896]{1,0:T(8,128)(2,1)} %refs_0_.1, bf16[896,896]{1,0:T(8,128)(2,1)} %refs_1_.2, bf16[1024,896]{1,0:T(8,128)(2,1)} %refs_2_.2, bf16[896,896]{1,0:T(8,128)(2,1)} %refs_3_.1), custom_call_target="tpu_custom_call" | custom-call | flops 6576668672 | bytes 11698176 | tf_op jit(solution)/shard_map/terms/pallas_call | solution.py:179
  13.4 0.1 collective-permute-start
  13.5 0.0 copy-start
  13.5 5.8 %all-to-all-start = ((bf16[8,112,896]{2,1,0:T(8,128)(2,1)}), bf16[8,112,896]{2,1,0:T(8,128)(2,1)S(1)}, u32[]{:S(2)}, u32[]{:S(2)}) async-start(bf16[8,112,896]{2,1,0:T(8,128)(2,1)} %bitcast.3), calls=%async_computation | async-start | bytes 3211264 | tf_op jit(solution)/shard_map/all_to_all | solution.py:225
  19.3 0.0 collective-permute-done.refs_1_
  19.3 0.0 copy-done
  19.4 1.6 %core_sum.1 = (f32[112,896]{1,0:T(8,128)S(1)}, bf16[112,896]{1,0:T(8,128)(2,1)S(1)}, bf16[112,896]{1,0:T(8,128)(2,1)S(1)}, bf16[112,896]{1,0:T(8,128)(2,1)S(1)}) custom-call(f32[448,896]{1,0:T(8,128)S(1)} %copy-done, f32[448,896]{1,0:T(8,128)} %collective-permute-done.refs_1_), custom_call_target="tpu_custom_call" | custom-call | bytes 4214784 | tf_op jit(solution)/shard_map/core_sum/pallas_call | solution.py:179
  20.9 0.3 collective-permute-start.1
  21.2 2.6 %collective-permute-start.2 = (bf16[112,896]{1,0:T(8,128)(2,1)S(1)}, bf16[112,896]{1,0:T(8,128)(2,1)S(1)}, u32[]{:S(2)}, u32[]{:S(2)}) collective-permute-start(bf16[112,896]{1,0:T(8,128)(2,1)S(1)} %get-tuple-element.30), channel_id=1, source_target_pairs={{0,4},{1,5},{2,6},{3,7},{4,0},{5,1},{6,2},{7,3},{8,12},{9,13},{10,... | collective-permute-start | bytes 602120 | tf_op jit(solution)/shard_map/ppermute | solution.py:203
  23.8 0.0 collective-permute-start.3
  23.8 5.0 %collective-permute-done.1.refs_1_ = bf16[112,896]{1,0:T(8,128)(2,1)S(1)} collective-permute-done((bf16[112,896]{1,0:T(8,128)(2,1)S(1)}, bf16[112,896]{1,0:T(8,128)(2,1)S(1)}, u32[]{:S(2)}, u32[]{:S(2)}) %collective-permute-start.1) | collective-permute-done | bytes 200736 | tf_op jit(solution)/shard_map/ppermute | solution.py:203
  28.8 1.8 %collective-permute-done.2.refs_2_ = bf16[112,896]{1,0:T(8,128)(2,1)S(1)} collective-permute-done((bf16[112,896]{1,0:T(8,128)(2,1)S(1)}, bf16[112,896]{1,0:T(8,128)(2,1)S(1)}, u32[]{:S(2)}, u32[]{:S(2)}) %collective-permute-start.2) | collective-permute-done | bytes 200736 | tf_op jit(solution)/shard_map/ppermute | solution.py:203
  30.6 3.4 %collective-permute-done.3.refs_3_ = bf16[112,896]{1,0:T(8,128)(2,1)S(1)} collective-permute-done((bf16[112,896]{1,0:T(8,128)(2,1)S(1)}, bf16[112,896]{1,0:T(8,128)(2,1)S(1)}, u32[]{:S(2)}, u32[]{:S(2)}) %collective-permute-start.3) | collective-permute-done | bytes 200736 | tf_op jit(solution)/shard_map/ppermute | solution.py:203
  34.0 0.9 %y_sum.1 = (f32[112,896]{1,0:T(8,128)S(1)}, f32[28,896]{1,0:T(8,128)S(1)}, f32[28,896]{1,0:T(8,128)}, bf16[28,896]{1,0:T(8,128)(2,1)}, f32[28,896]{1,0:T(8,128)S(1)}) custom-call(f32[112,896]{1,0:T(8,128)S(1)} %get-tuple-element.28.refs_0_, bf16[112,896]{1,0:T(8,128)(2,1)S(1)} %collective-permute-done.1.refs_1_, ...), custom_call_target="tpu_custom_call" | custom-call | flops 15000000512 | bytes 1756160 | tf_op jit(solution)/shard_map/y_sum/pallas_call | solution.py:179
  34.9 3.3 %collective-permute-start.4 = (f32[28,896]{1,0:T(8,128)}, f32[28,896]{1,0:T(8,128)S(1)}, u32[]{:S(2)}, u32[]{:S(2)}) collective-permute-start(f32[28,896]{1,0:T(8,128)} %get-tuple-element.33), channel_id=1, source_target_pairs={{0,8},{1,9},{2,10},{3,11},{4,12},{5,13},{6,14},{7,15},{8,16},{9,17... | collective-permute-start | bytes 301064 | tf_op jit(solution)/shard_map/ppermute | solution.py:203
  38.2 2.4 %collective-permute-start.6 = (f32[28,896]{1,0:T(8,128)S(1)}, f32[28,896]{1,0:T(8,128)S(1)}, u32[]{:S(2)}, u32[]{:S(2)}) collective-permute-start(f32[28,896]{1,0:T(8,128)S(1)} %get-tuple-element.35), channel_id=1, source_target_pairs={{0,24},{1,25},{2,26},{3,27},{4,28},{5,29},{6,30},{7,31},{8,0},{9,1... | collective-permute-start | bytes 301064 | tf_op jit(solution)/shard_map/ppermute | solution.py:203
  40.6 4.8 %collective-permute-start.5 = (bf16[28,896]{1,0:T(8,128)(2,1)}, bf16[28,896]{1,0:T(8,128)(2,1)S(1)}, u32[]{:S(2)}, u32[]{:S(2)}) collective-permute-start(bf16[28,896]{1,0:T(8,128)(2,1)} %get-tuple-element.34), channel_id=1, source_target_pairs={{0,16},{1,17},{2,18},{3,19},{4,20},{5,21},{6,22},{7,23},{8,24},{9,... | collective-permute-start | bytes 150536 | tf_op jit(solution)/shard_map/ppermute | solution.py:203
  45.3 0.0 all-to-all-done.refs_0_
  45.3 1.7 %update_second.1 = (f32[112,896]{1,0:T(8,128)}, f32[112,896]{1,0:T(8,128)}, bf16[8,112,896]{2,1,0:T(8,128)(2,1)}) custom-call(bf16[8,112,896]{2,1,0:T(8,128)(2,1)S(1)} %all-to-all-done.refs_0_, f32[112,896]{1,0:T(8,128)S(1)} %copy-done.1, f32[112,896]{1,0:T(8,128)S(1)} %copy-done.2, f32[112,896]{1,0:T(8,128)S(1)} %get-tuple-element.37.refs_3_), custom_call_target="tpu_custom_call" | custom-call | bytes 4816896 | tf_op jit(solution)/shard_map/update_second/pallas_call | solution.py:179
  47.0 3.8 %collective-permute-done.5.refs_2_ = bf16[28,896]{1,0:T(8,128)(2,1)S(1)} collective-permute-done((bf16[28,896]{1,0:T(8,128)(2,1)}, bf16[28,896]{1,0:T(8,128)(2,1)S(1)}, u32[]{:S(2)}, u32[]{:S(2)}) %collective-permute-start.5) | collective-permute-done | bytes 50208 | tf_op jit(solution)/shard_map/ppermute | solution.py:203
  50.9 0.0 collective-permute-done.4.refs_1_
  50.9 0.0 collective-permute-done.6.refs_3_
  50.9 0.0 copy-done.3
  50.9 0.7 update_first.1
  51.6 1.9 %collective-permute-start.9 = (bf16[28,896]{1,0:T(8,128)(2,1)S(1)}, bf16[28,896]{1,0:T(8,128)(2,1)S(1)}, u32[]{:S(2)}, u32[]{:S(2)}) collective-permute-start(bf16[28,896]{1,0:T(8,128)(2,1)S(1)} %get-tuple-element.43.refs_0_), channel_id=1, source_target_pairs={{0,24},{1,25},{2,26},{3,27},{4,28},{5,29},{6,30},{7,31},{8,0},{9,1... | collective-permute-start | bytes 150536 | tf_op jit(solution)/shard_map/ppermute | solution.py:203
  53.5 4.0 %collective-permute-start.8 = (bf16[28,896]{1,0:T(8,128)(2,1)S(1)}, bf16[28,896]{1,0:T(8,128)(2,1)S(1)}, u32[]{:S(2)}, u32[]{:S(2)}) collective-permute-start(bf16[28,896]{1,0:T(8,128)(2,1)S(1)} %get-tuple-element.43.refs_0_), channel_id=1, source_target_pairs={{0,16},{1,17},{2,18},{3,19},{4,20},{5,21},{6,22},{7,23},{8,24},{9,... | collective-permute-start | bytes 150536 | tf_op jit(solution)/shard_map/ppermute | solution.py:203
  57.5 0.0 collective-permute-start.7
  57.5 6.0 %all-to-all-start.1 = ((bf16[8,112,896]{2,1,0:T(8,128)(2,1)}), bf16[8,112,896]{2,1,0:T(8,128)(2,1)S(1)}, u32[]{:S(2)}, u32[]{:S(2)}) async-start(bf16[8,112,896]{2,1,0:T(8,128)(2,1)} %get-tuple-element.38.refs_6_), calls=%async_computation.1 | async-start | bytes 3211264 | tf_op jit(solution)/shard_map/all_to_all | solution.py:265
  63.5 0.0 collective-permute-done.9.refs_3_
  63.5 0.0 collective-permute-done.8.refs_2_
  63.5 1.0 %collective-permute-done.7.refs_1_ = bf16[28,896]{1,0:T(8,128)(2,1)S(1)} collective-permute-done((bf16[28,896]{1,0:T(8,128)(2,1)S(1)}, bf16[28,896]{1,0:T(8,128)(2,1)S(1)}, u32[]{:S(2)}, u32[]{:S(2)}) %collective-permute-start.7) | collective-permute-done | bytes 50208 | tf_op jit(solution)/shard_map/ppermute | solution.py:203
  64.5 0.1 join_z.1.p0
  64.7 0.5 collective-permute-start.12
  65.1 1.4 %collective-permute-start.11 = (bf16[112,896]{1,0:T(8,128)(2,1)S(1)}, bf16[112,896]{1,0:T(8,128)(2,1)S(1)}, u32[]{:S(2)}, u32[]{:S(2)}) collective-permute-start(bf16[112,896]{1,0:T(8,128)(2,1)S(1)} %join_z.1.p0), channel_id=1, source_target_pairs={{0,4},{1,5},{2,6},{3,7},{4,0},{5,1},{6,2},{7,3},{8,12},{9,13},{10,... | collective-permute-start | bytes 602120 | tf_op jit(solution)/shard_map/ppermute | solution.py:203
  66.6 1.9 %collective-permute-start.10 = (bf16[112,896]{1,0:T(8,128)(2,1)S(1)}, bf16[112,896]{1,0:T(8,128)(2,1)S(1)}, u32[]{:S(2)}, u32[]{:S(2)}) collective-permute-start(bf16[112,896]{1,0:T(8,128)(2,1)S(1)} %join_z.1.p0), channel_id=1, source_target_pairs={{0,2},{1,3},{2,4},{3,5},{4,6},{5,7},{6,0},{7,1},{8,10},{9,11},{10,... | collective-permute-start | bytes 602120 | tf_op jit(solution)/shard_map/ppermute | solution.py:203
  68.4 0.0 collective-permute-start.13
  68.4 5.6 %collective-permute-done.12.p3 = bf16[112,896]{1,0:T(8,128)(2,1)S(1)} collective-permute-done((bf16[112,896]{1,0:T(8,128)(2,1)S(1)}, bf16[112,896]{1,0:T(8,128)(2,1)S(1)}, u32[]{:S(2)}, u32[]{:S(2)}) %collective-permute-start.12) | collective-permute-done | bytes 200736 | tf_op jit(solution)/shard_map/ppermute | solution.py:203
  74.0 0.0 collective-permute-start.16
  74.0 0.0 collective-permute-done.11.p2
  74.0 0.5 collective-permute-start.15
  74.5 0.2 collective-permute-done.10.p1
  74.7 0.0 collective-permute-start.14
  74.7 0.0 collective-permute-done.13.q0
  74.7 0.7 collective-permute-done.16.q3
  75.5 0.3 collective-permute-done.15.q2
  75.7 0.4 collective-permute-done.14.q1
  76.2 6.4 %all-to-all-done.1 = bf16[8,112,896]{2,1,0:T(8,128)(2,1)S(1)} async-done(((bf16[8,112,896]{2,1,0:T(8,128)(2,1)}), bf16[8,112,896]{2,1,0:T(8,128)(2,1)S(1)}, u32[]{:S(2)}, u32[]{:S(2)}) %all-to-all-start.1) | async-done | bytes 1605664 | tf_op jit(solution)/shard_map/all_to_all | solution.py:265
  82.5 2.5 %join.1 = (bf16[896,896]{1,0:T(8,128)(2,1)}, bf16[896,896]{1,0:T(8,128)(2,1)}) custom-call(bf16[112,896]{1,0:T(8,128)(2,1)S(1)} %join_z.1.p0, bf16[112,896]{1,0:T(8,128)(2,1)S(1)} %collective-permute-done.10.p1, bf16[112,896]{1,0:T(8,128)(2,1)S(1)} %collective-permute-done.11.p2, bf16[112,896]{1,0:T(8,128)(2,1)S(1)} %collective-permute-done.12.p3, ...), custom_call_target="tpu_custom_call" | custom-call | bytes 6422528 | tf_op jit(solution)/shard_map/join/pallas_call | solution.py:270
  (7 shorter events, 0.0 us)
Async XLA Ops:
  13.4 5.9 %collective-permute-start = (f32[448,896]{1,0:T(8,128)}, f32[448,896]{1,0:T(8,128)}, u32[]{:S(2)}, u32[]{:S(2)}) collective-permute-start(f32[448,896]{1,0:T(8,128)} %get-tuple-element.27), channel_id=1, source_target_pairs={{0,1},{1,0},{2,3},{3,2},{4,5},{5,4},{6,7},{7,6},{8,9},{9,8},{10,11... | collective-permute-start | bytes 4816904 | tf_op jit(solution)/shard_map/ppermute | solution.py:203
  13.5 5.8 %copy-start = (f32[448,896]{1,0:T(8,128)S(1)}, f32[448,896]{1,0:T(8,128)}, u32[]{:S(2)}) copy-start(f32[448,896]{1,0:T(8,128)} %get-tuple-element.26.refs_0_) | copy-start | bytes 4816900
  13.5 31.8 %all-to-all-start = ((bf16[8,112,896]{2,1,0:T(8,128)(2,1)}), bf16[8,112,896]{2,1,0:T(8,128)(2,1)S(1)}, u32[]{:S(2)}, u32[]{:S(2)}) async-start(bf16[8,112,896]{2,1,0:T(8,128)(2,1)} %bitcast.3), calls=%async_computation | async-start | bytes 3211264 | tf_op jit(solution)/shard_map/all_to_all | solution.py:225
  20.9 7.9 %collective-permute-start.1 = (bf16[112,896]{1,0:T(8,128)(2,1)S(1)}, bf16[112,896]{1,0:T(8,128)(2,1)S(1)}, u32[]{:S(2)}, u32[]{:S(2)}) collective-permute-start(bf16[112,896]{1,0:T(8,128)(2,1)S(1)} %get-tuple-element.29), channel_id=1, source_target_pairs={{0,2},{1,3},{2,4},{3,5},{4,6},{5,7},{6,0},{7,1},{8,10},{9,11},{10,... | collective-permute-start | bytes 602120 | tf_op jit(solution)/shard_map/ppermute | solution.py:203
  21.2 9.4 %collective-permute-start.2 = (bf16[112,896]{1,0:T(8,128)(2,1)S(1)}, bf16[112,896]{1,0:T(8,128)(2,1)S(1)}, u32[]{:S(2)}, u32[]{:S(2)}) collective-permute-start(bf16[112,896]{1,0:T(8,128)(2,1)S(1)} %get-tuple-element.30), channel_id=1, source_target_pairs={{0,4},{1,5},{2,6},{3,7},{4,0},{5,1},{6,2},{7,3},{8,12},{9,13},{10,... | collective-permute-start | bytes 602120 | tf_op jit(solution)/shard_map/ppermute | solution.py:203
  23.8 10.2 %collective-permute-start.3 = (bf16[112,896]{1,0:T(8,128)(2,1)S(1)}, bf16[112,896]{1,0:T(8,128)(2,1)S(1)}, u32[]{:S(2)}, u32[]{:S(2)}) collective-permute-start(bf16[112,896]{1,0:T(8,128)(2,1)S(1)} %get-tuple-element.31), channel_id=1, source_target_pairs={{0,6},{1,7},{2,0},{3,1},{4,2},{5,3},{6,4},{7,5},{8,14},{9,15},{10,... | collective-permute-start | bytes 602120 | tf_op jit(solution)/shard_map/ppermute | solution.py:203
  34.0 11.3 %copy-start.1 = (f32[112,896]{1,0:T(8,128)S(1)}, f32[112,896]{1,0:T(8,128)}, u32[]{:S(2)}) copy-start(f32[112,896]{1,0:T(8,128)} %refs_1_.3) | copy-start | bytes 1204228
  34.0 11.3 %copy-start.2 = (f32[112,896]{1,0:T(8,128)S(1)}, f32[112,896]{1,0:T(8,128)}, u32[]{:S(2)}) copy-start(f32[112,896]{1,0:T(8,128)} %refs_2_.3) | copy-start | bytes 1204228
  34.9 16.0 %copy-start.3 = (f32[28,896]{1,0:T(8,128)S(1)}, f32[28,896]{1,0:T(8,128)}, u32[]{:S(2)}) copy-start(f32[28,896]{1,0:T(8,128)} %refs_4_.1) | copy-start | bytes 301060
  34.9 16.0 %copy-start.4 = (f32[28,896]{1,0:T(8,128)S(1)}, f32[28,896]{1,0:T(8,128)}, u32[]{:S(2)}) copy-start(f32[28,896]{1,0:T(8,128)} %refs_5_.1) | copy-start | bytes 301060
  34.9 16.0 %collective-permute-start.4 = (f32[28,896]{1,0:T(8,128)}, f32[28,896]{1,0:T(8,128)S(1)}, u32[]{:S(2)}, u32[]{:S(2)}) collective-permute-start(f32[28,896]{1,0:T(8,128)} %get-tuple-element.33), channel_id=1, source_target_pairs={{0,8},{1,9},{2,10},{3,11},{4,12},{5,13},{6,14},{7,15},{8,16},{9,17... | collective-permute-start | bytes 301064 | tf_op jit(solution)/shard_map/ppermute | solution.py:203
  38.2 12.7 %collective-permute-start.6 = (f32[28,896]{1,0:T(8,128)S(1)}, f32[28,896]{1,0:T(8,128)S(1)}, u32[]{:S(2)}, u32[]{:S(2)}) collective-permute-start(f32[28,896]{1,0:T(8,128)S(1)} %get-tuple-element.35), channel_id=1, source_target_pairs={{0,24},{1,25},{2,26},{3,27},{4,28},{5,29},{6,30},{7,31},{8,0},{9,1... | collective-permute-start | bytes 301064 | tf_op jit(solution)/shard_map/ppermute | solution.py:203
  40.6 10.3 %collective-permute-start.5 = (bf16[28,896]{1,0:T(8,128)(2,1)}, bf16[28,896]{1,0:T(8,128)(2,1)S(1)}, u32[]{:S(2)}, u32[]{:S(2)}) collective-permute-start(bf16[28,896]{1,0:T(8,128)(2,1)} %get-tuple-element.34), channel_id=1, source_target_pairs={{0,16},{1,17},{2,18},{3,19},{4,20},{5,21},{6,22},{7,23},{8,24},{9,... | collective-permute-start | bytes 150536 | tf_op jit(solution)/shard_map/ppermute | solution.py:203
  51.6 11.9 %collective-permute-start.9 = (bf16[28,896]{1,0:T(8,128)(2,1)S(1)}, bf16[28,896]{1,0:T(8,128)(2,1)S(1)}, u32[]{:S(2)}, u32[]{:S(2)}) collective-permute-start(bf16[28,896]{1,0:T(8,128)(2,1)S(1)} %get-tuple-element.43.refs_0_), channel_id=1, source_target_pairs={{0,24},{1,25},{2,26},{3,27},{4,28},{5,29},{6,30},{7,31},{8,0},{9,1... | collective-permute-start | bytes 150536 | tf_op jit(solution)/shard_map/ppermute | solution.py:203
  53.5 10.0 %collective-permute-start.8 = (bf16[28,896]{1,0:T(8,128)(2,1)S(1)}, bf16[28,896]{1,0:T(8,128)(2,1)S(1)}, u32[]{:S(2)}, u32[]{:S(2)}) collective-permute-start(bf16[28,896]{1,0:T(8,128)(2,1)S(1)} %get-tuple-element.43.refs_0_), channel_id=1, source_target_pairs={{0,16},{1,17},{2,18},{3,19},{4,20},{5,21},{6,22},{7,23},{8,24},{9,... | collective-permute-start | bytes 150536 | tf_op jit(solution)/shard_map/ppermute | solution.py:203
  57.5 7.0 %collective-permute-start.7 = (bf16[28,896]{1,0:T(8,128)(2,1)S(1)}, bf16[28,896]{1,0:T(8,128)(2,1)S(1)}, u32[]{:S(2)}, u32[]{:S(2)}) collective-permute-start(bf16[28,896]{1,0:T(8,128)(2,1)S(1)} %get-tuple-element.43.refs_0_), channel_id=1, source_target_pairs={{0,8},{1,9},{2,10},{3,11},{4,12},{5,13},{6,14},{7,15},{8,16},{9,17... | collective-permute-start | bytes 150536 | tf_op jit(solution)/shard_map/ppermute | solution.py:203
  57.5 25.0 %all-to-all-start.1 = ((bf16[8,112,896]{2,1,0:T(8,128)(2,1)}), bf16[8,112,896]{2,1,0:T(8,128)(2,1)S(1)}, u32[]{:S(2)}, u32[]{:S(2)}) async-start(bf16[8,112,896]{2,1,0:T(8,128)(2,1)} %get-tuple-element.38.refs_6_), calls=%async_computation.1 | async-start | bytes 3211264 | tf_op jit(solution)/shard_map/all_to_all | solution.py:265
  64.7 9.3 %collective-permute-start.12 = (bf16[112,896]{1,0:T(8,128)(2,1)S(1)}, bf16[112,896]{1,0:T(8,128)(2,1)S(1)}, u32[]{:S(2)}, u32[]{:S(2)}) collective-permute-start(bf16[112,896]{1,0:T(8,128)(2,1)S(1)} %join_z.1.p0), channel_id=1, source_target_pairs={{0,6},{1,7},{2,0},{3,1},{4,2},{5,3},{6,4},{7,5},{8,14},{9,15},{10,... | collective-permute-start | bytes 602120 | tf_op jit(solution)/shard_map/ppermute | solution.py:203
  65.1 8.9 %collective-permute-start.11 = (bf16[112,896]{1,0:T(8,128)(2,1)S(1)}, bf16[112,896]{1,0:T(8,128)(2,1)S(1)}, u32[]{:S(2)}, u32[]{:S(2)}) collective-permute-start(bf16[112,896]{1,0:T(8,128)(2,1)S(1)} %join_z.1.p0), channel_id=1, source_target_pairs={{0,4},{1,5},{2,6},{3,7},{4,0},{5,1},{6,2},{7,3},{8,12},{9,13},{10,... | collective-permute-start | bytes 602120 | tf_op jit(solution)/shard_map/ppermute | solution.py:203
  66.6 8.1 %collective-permute-start.10 = (bf16[112,896]{1,0:T(8,128)(2,1)S(1)}, bf16[112,896]{1,0:T(8,128)(2,1)S(1)}, u32[]{:S(2)}, u32[]{:S(2)}) collective-permute-start(bf16[112,896]{1,0:T(8,128)(2,1)S(1)} %join_z.1.p0), channel_id=1, source_target_pairs={{0,2},{1,3},{2,4},{3,5},{4,6},{5,7},{6,0},{7,1},{8,10},{9,11},{10,... | collective-permute-start | bytes 602120 | tf_op jit(solution)/shard_map/ppermute | solution.py:203
  68.4 6.3 %collective-permute-start.13 = (bf16[112,896]{1,0:T(8,128)(2,1)S(1)}, bf16[112,896]{1,0:T(8,128)(2,1)S(1)}, u32[]{:S(2)}, u32[]{:S(2)}) collective-permute-start(bf16[112,896]{1,0:T(8,128)(2,1)S(1)} %join_z.1.p0), channel_id=1, source_target_pairs={{0,1},{1,0},{2,3},{3,2},{4,5},{5,4},{6,7},{7,6},{8,9},{9,8},{10,11... | collective-permute-start | bytes 602120 | tf_op jit(solution)/shard_map/ppermute | solution.py:203
  74.0 1.4 %collective-permute-start.16 = (bf16[112,896]{1,0:T(8,128)(2,1)S(1)}, bf16[112,896]{1,0:T(8,128)(2,1)S(1)}, u32[]{:S(2)}, u32[]{:S(2)}) collective-permute-start(bf16[112,896]{1,0:T(8,128)(2,1)S(1)} %collective-permute-done.12.p3), channel_id=1, source_target_pairs={{0,1},{1,0},{2,3},{3,2},{4,5},{5,4},{6,7},{7,6},{8,9},{9,8},{10,11... | collective-permute-start | bytes 602120 | tf_op jit(solution)/shard_map/ppermute | solution.py:203
  74.0 1.7 %collective-permute-start.15 = (bf16[112,896]{1,0:T(8,128)(2,1)S(1)}, bf16[112,896]{1,0:T(8,128)(2,1)S(1)}, u32[]{:S(2)}, u32[]{:S(2)}) collective-permute-start(bf16[112,896]{1,0:T(8,128)(2,1)S(1)} %collective-permute-done.11.p2), channel_id=1, source_target_pairs={{0,1},{1,0},{2,3},{3,2},{4,5},{5,4},{6,7},{7,6},{8,9},{9,8},{10,11... | collective-permute-start | bytes 602120 | tf_op jit(solution)/shard_map/ppermute | solution.py:203
  74.7 1.4 %collective-permute-start.14 = (bf16[112,896]{1,0:T(8,128)(2,1)S(1)}, bf16[112,896]{1,0:T(8,128)(2,1)S(1)}, u32[]{:S(2)}, u32[]{:S(2)}) collective-permute-start(bf16[112,896]{1,0:T(8,128)(2,1)S(1)} %collective-permute-done.10.p1), channel_id=1, source_target_pairs={{0,1},{1,0},{2,3},{3,2},{4,5},{5,4},{6,7},{7,6},{8,9},{9,8},{10,11... | collective-permute-start | bytes 602120 | tf_op jit(solution)/shard_map/ppermute | solution.py:203

commit v4 on v3

--- a/solution.py
+++ b/solution.py
@@ -59,7 +59,9 @@
     return (outer_new, moment_new)
 
 
-def terms_kernel(x_hbm, w1_hbm, g_hbm, w2_hbm, mine, theirs, second, x, w1, g, w2, s, fc, acc, sems):
+def terms_kernel(
+    x_hbm, w1_hbm, g_hbm, w2_hbm, mine, theirs, second_hbm, x, w1, g, w2, s, fc, acc, halves, second, sems
+):
     def fetch(src, dst, i):
         return pltpu.make_async_copy(src, dst, sems.at[i])
 
@@ -85,20 +87,26 @@
         get_g[t].wait()
         backward = dot(g[rows, :], w2[...], 1, 1) * UNIT
         fc[rows, :] = (backward * logistic * (1.0 + hidden * (1.0 - logistic))).astype(BF16)
-    for r in range(D // RB):
-        cols = pl.ds(r * RB, RB)
+    tiles = [pl.ds(r * RB, RB) for r in range(D // RB)]
+    for cols in tiles:
         acc[cols, :] = w1[cols, :].astype(F32) - inner_rate * UNIT * dot(x[:, cols], fc[...], 0, 0)
-        grad_second = UNIT * dot(s[:, cols], g[...], 0, 0)
-        second[cols, :] = (w2[cols, :].astype(F32) - inner_rate * grad_second).astype(BF16)
     core = place()[2]
     for z in range(ZS):
         for y in range(YS):
             first = (z * YS + y) * CORES * SUB
-            even = acc[pl.ds(first, SUB), :]
-            odd = acc[pl.ds(first + SUB, SUB), :]
             rows = pl.ds(BLK * y + SUB * z, SUB)
-            mine[rows, :] = jnp.where(core == 0, even, odd)
-            theirs[rows, :] = jnp.where(core == 0, odd, even)
+            halves[core, rows, :] = acc[pl.ds(first, SUB), :]
+            halves[1 - core, rows, :] = acc[pl.ds(first + SUB, SUB), :]
+    puts = [fetch(halves.at[1], theirs, 0), fetch(halves.at[0], mine, 1)]
+    for copy in puts:
+        copy.start()
+    for r, cols in enumerate(tiles):
+        grad_second = UNIT * dot(s[:, cols], g[...], 0, 0)
+        second[cols, :] = (w2[cols, :].astype(F32) - inner_rate * grad_second).astype(BF16)
+        puts.append(fetch(second.at[cols], second_hbm.at[cols], 2 + r))
+        puts[-1].start()
+    for copy in puts:
+        copy.wait()
 
 
 def core_sum_kernel(mine, got, own, *sends):
@@ -112,7 +120,7 @@
             sends[k - 1][...] = block.astype(BF16)
 
 
-def y_sum_kernel(own, r1, r2, r3, total, o0, o1, o2, o3):
+def y_sum_kernel(own, r1, r2, r3, o0, o1, o2, o3, total):
     z = place()[0]
     total[...] = own[...] + r1[...].astype(F32) + r2[...].astype(F32) + r3[...].astype(F32)
     for k, out in enumerate((o0, o1, o2, o3)):
@@ -136,19 +144,24 @@
     out[...] = wide[...].astype(BF16)
 
 
-def join_kernel(p0, p1, p2, p3, q0, q1, q2, q3, second, out, second_out, wide, sems):
-    copies = [pltpu.make_async_copy(second, second_out, sems.at[0])]
-    for copy in copies:
-        copy.start()
+def join_kernel(p0, p1, p2, p3, q0, q1, q2, q3, out, wide, low, sems):
     _, y, core = place()
+    sides = []
     for j in range(YS):
         k = lax.rem(y - j + YS, YS)
         own = pick(k, [p[...] for p in (p0, p1, p2, p3)]).astype(F32)
         other = pick(k, [q[...] for q in (q0, q1, q2, q3)]).astype(F32)
-        for c, block in enumerate((jnp.where(core == 0, own, other), jnp.where(core == 0, other, own))):
-            for z in range(ZS):
-                wide[pl.ds(((z * YS + j) * CORES + c) * SUB, SUB), :] = block[z * SUB : (z + 1) * SUB]
-    out[...] = wide[...].astype(BF16)
+        sides.append((jnp.where(core == 0, own, other), jnp.where(core == 0, other, own)))
+    copies = []
+    for z in range(ZS):
+        for j in range(YS):
+            for c in range(CORES):
+                rows = pl.ds(((z * YS + j) * CORES + c) * SUB, SUB)
+                wide[rows, :] = sides[j][c][z * SUB : (z + 1) * SUB]
+        part = pl.ds(z * YS * CORES * SUB, YS * CORES * SUB)
+        low[part, :] = wide[part, :].astype(BF16)
+        copies.append(pltpu.make_async_copy(low.at[part], out.at[part], sems.at[z]))
+        copies[-1].start()
     for copy in copies:
         copy.wait()
 
@@ -165,7 +178,7 @@
         spread[k] = low
 
 
-def call(kernel, args, outs, scratch=(), flops=0, name=None, hbm_args=None, after=(), vmem=VMEM_BYTES):
+def call(kernel, args, outs, scratch=(), flops=0, name=None, hbm_args=None, after=(), vmem=VMEM_BYTES, hbm_outs=False):
     inside = pl.BlockSpec(memory_space=pltpu.VMEM)
     outside = pl.BlockSpec(memory_space=pltpu.HBM)
     shapes = tuple(jax.ShapeDtypeStruct(shape, dtype) for shape, dtype in outs)
@@ -181,7 +194,7 @@
         out_shape=shapes,
         in_specs=[outside if h else inside for h in (hbm_args or [False] * len(args))]
         + [pl.BlockSpec(memory_space=pl.ANY) for _ in after],
-        out_specs=tuple(inside for _ in shapes),
+        out_specs=tuple(outside if hbm_outs else inside for _ in shapes),
         scratch_shapes=list(scratch),
         compiler_params=pltpu.CompilerParams(vmem_limit_bytes=vmem),
         cost_estimate=pl.CostEstimate(flops=flops, bytes_accessed=moved, transcendentals=0),
@@ -214,9 +227,12 @@
             pltpu.VMEM((T, D), BF16),
             pltpu.VMEM((T, D), BF16),
             pltpu.VMEM((D, D), F32),
+            pltpu.VMEM((CORES, D // 2, D), F32),
+            pltpu.VMEM((D, D), BF16),
             pltpu.SemaphoreType.DMA((2 + 2 * (T // TB),)),
         ],
         flops=8 * T * D * D,
+        hbm_outs=True,
         name="terms",
         hbm_args=(True,) * 4,
         vmem=MOST_VMEM,
@@ -231,10 +247,11 @@
         name="core_sum",
     )
     y_terms = [send(s, 0, k + 1, 0) for k, s in enumerate(sends)]
-    y_total, own, *sends = call(
+    own, *sends = call(
         y_sum_kernel,
         (own, *y_terms),
-        (((BLK, D), F32),) + tuple(((SUB, D), t) for t in (F32, F32, BF16, F32)),
+        tuple(((SUB, D), t) for t in (F32, F32, BF16, F32)),
+        [pltpu.VMEM((BLK, D), F32)],
         flops=SOME,
         name="y_sum",
     )
@@ -244,7 +261,7 @@
         (terms_second, outer_second, momentum_second),
         (((SUB2, D), F32), ((SUB2, D), F32), ((ROWS, SUB2, D), BF16)),
         name="update_second",
-        after=(y_total,),
+        after=(own,),
     )
     new_outer_first, new_momentum_first, low = call(
         update_first_kernel,
@@ -262,21 +279,17 @@
         flops=LONG,
         name="join_z",
     )
-    gathered_second = lax.all_to_all(spread, "row", 0, 0)
+    reset_second = lax.all_to_all(spread, "row", 0, 0).reshape(D, D)
     blocks = [block] + [send(block, 0, k, 0) for k in range(1, YS)]
     others = [send(b, 0, 0, 1) for b in blocks]
-    vmem, anywhere = pl.BlockSpec(memory_space=pltpu.VMEM), pl.BlockSpec(memory_space=pl.ANY)
-    module = jax.ShapeDtypeStruct((D, D), BF16)
-    reset_first, reset_second = pl.pallas_call(
+    (reset_first,) = call(
         join_kernel,
-        out_shape=(module, module),
-        in_specs=[vmem] * 8 + [anywhere],
-        out_specs=(vmem, anywhere),
-        scratch_shapes=[pltpu.VMEM((D, D), F32), pltpu.SemaphoreType.DMA((1,))],
-        compiler_params=pltpu.CompilerParams(vmem_limit_bytes=VMEM_BYTES),
-        cost_estimate=pl.CostEstimate(flops=0, bytes_accessed=8 * D * D, transcendentals=0),
+        (*blocks, *others),
+        (((D, D), BF16),),
+        [pltpu.VMEM((D, D), F32), pltpu.VMEM((D, D), BF16), pltpu.SemaphoreType.DMA((ZS,))],
         name="join",
-    )(*blocks, *others, gathered_second.reshape(D, D))
+        hbm_outs=True,
+    )
     return (
         new_outer_first,
         new_momentum_first,

time: 85.4 us -> 83.3 us (0.975)
  the two profiles are of different devices: /device:TPU:24 before, /device:TPU:1 now
where the time goes in v4:
time: 83.3 us; the launch traced here: 82.7 us
  starting transfers between devices  46.2 us (55%)
  Pallas kernels  18.9 us (23%)
  waiting for transfers between devices  15.6 us (19%)
  local copies, waits for them, and re-layouts  1.18 us (1%)
    ppermute x17, starting transfers between devices, send(): return lax.ppermute(value, 'col', shift(dz, dy, dc))  38.3 us
    pallas_call x7, Pallas kernels, call(): pl.pallas_call(body, out_shape=shapes, in_specs=[outside if h else inside...  18.9 us
    ppermute x17, waiting for transfers between devices, send(): return lax.ppermute(value, 'col', shift(dz, dy, dc))  15.6 us
    all_to_all x1, starting transfers between devices, on_device(): reset_second = lax.all_to_all(spread, 'row', 0, 0).reshape(D, D)  4.09 us
    all_to_all x1, starting transfers between devices, on_device(): lax.all_to_all(final_second.reshape(ROWS, SUB2, D), 'row', 0, 0)  3.77 us
  transfers between devices with their start and end apart: 19, of which 7 were waited for; matrix products, arithmetic and copies ran while one was open for 0% of the time, Pallas kernels for 7%

profile of v4, /device:TPU:1, one launch (start us, length us, event | category | flops | bytes accessed | tf_op | source)
XLA Modules:
  0.0 82.7 jit_solution(1974818365063578243)
XLA Ops:
  0.6 12.4 %terms.1 = (f32[448,896]{1,0:T(8,128)}, f32[448,896]{1,0:T(8,128)}, bf16[896,896]{1,0:T(8,128)(2,1)}) custom-call(bf16[1024,896]{1,0:T(8,128)(2,1)} %refs_0_.1, bf16[896,896]{1,0:T(8,128)(2,1)} %refs_1_.2, bf16[1024,896]{1,0:T(8,128)(2,1)} %refs_2_.2, bf16[896,896]{1,0:T(8,128)(2,1)} %refs_3_.1), custom_call_target="tpu_custom_call" | custom-call | flops 6576668672 | bytes 11698176 | tf_op jit(solution)/shard_map/terms/pallas_call | solution.py:192
  13.0 3.3 %collective-permute-start = (f32[448,896]{1,0:T(8,128)}, f32[448,896]{1,0:T(8,128)}, u32[]{:S(2)}, u32[]{:S(2)}) collective-permute-start(f32[448,896]{1,0:T(8,128)} %get-tuple-element.24), channel_id=1, source_target_pairs={{0,1},{1,0},{2,3},{3,2},{4,5},{5,4},{6,7},{7,6},{8,9},{9,8},{10,11... | collective-permute-start | bytes 4816904 | tf_op jit(solution)/shard_map/ppermute | solution.py:216
  16.3 3.8 %all-to-all-start = ((bf16[8,112,896]{2,1,0:T(8,128)(2,1)}), bf16[8,112,896]{2,1,0:T(8,128)(2,1)S(1)}, u32[]{:S(2)}, u32[]{:S(2)}) async-start(bf16[8,112,896]{2,1,0:T(8,128)(2,1)} %bitcast.3), calls=%async_computation | async-start | bytes 3211264 | tf_op jit(solution)/shard_map/all_to_all | solution.py:241
  20.1 0.0 collective-permute-done.refs_1_
  20.1 1.6 %core_sum.1 = (f32[112,896]{1,0:T(8,128)S(1)}, bf16[112,896]{1,0:T(8,128)(2,1)S(1)}, bf16[112,896]{1,0:T(8,128)(2,1)S(1)}, bf16[112,896]{1,0:T(8,128)(2,1)S(1)}) custom-call(f32[448,896]{1,0:T(8,128)S(1)} %copy-done, f32[448,896]{1,0:T(8,128)} %collective-permute-done.refs_1_), custom_call_target="tpu_custom_call" | custom-call | bytes 4214784 | tf_op jit(solution)/shard_map/core_sum/pallas_call | solution.py:192
  21.7 1.4 %collective-permute-start.1 = (bf16[112,896]{1,0:T(8,128)(2,1)S(1)}, bf16[112,896]{1,0:T(8,128)(2,1)S(1)}, u32[]{:S(2)}, u32[]{:S(2)}) collective-permute-start(bf16[112,896]{1,0:T(8,128)(2,1)S(1)} %get-tuple-element.26), channel_id=1, source_target_pairs={{0,2},{1,3},{2,4},{3,5},{4,6},{5,7},{6,0},{7,1},{8,10},{9,11},{10,... | collective-permute-start | bytes 602120 | tf_op jit(solution)/shard_map/ppermute | solution.py:216
  23.1 2.6 %collective-permute-start.2 = (bf16[112,896]{1,0:T(8,128)(2,1)S(1)}, bf16[112,896]{1,0:T(8,128)(2,1)S(1)}, u32[]{:S(2)}, u32[]{:S(2)}) collective-permute-start(bf16[112,896]{1,0:T(8,128)(2,1)S(1)} %get-tuple-element.27), channel_id=1, source_target_pairs={{0,4},{1,5},{2,6},{3,7},{4,0},{5,1},{6,2},{7,3},{8,12},{9,13},{10,... | collective-permute-start | bytes 602120 | tf_op jit(solution)/shard_map/ppermute | solution.py:216
  25.7 1.1 %collective-permute-start.3 = (bf16[112,896]{1,0:T(8,128)(2,1)S(1)}, bf16[112,896]{1,0:T(8,128)(2,1)S(1)}, u32[]{:S(2)}, u32[]{:S(2)}) collective-permute-start(bf16[112,896]{1,0:T(8,128)(2,1)S(1)} %get-tuple-element.28), channel_id=1, source_target_pairs={{0,6},{1,7},{2,0},{3,1},{4,2},{5,3},{6,4},{7,5},{8,14},{9,15},{10,... | collective-permute-start | bytes 602120 | tf_op jit(solution)/shard_map/ppermute | solution.py:216
  26.7 2.6 %collective-permute-done.1.refs_1_ = bf16[112,896]{1,0:T(8,128)(2,1)S(1)} collective-permute-done((bf16[112,896]{1,0:T(8,128)(2,1)S(1)}, bf16[112,896]{1,0:T(8,128)(2,1)S(1)}, u32[]{:S(2)}, u32[]{:S(2)}) %collective-permute-start.1) | collective-permute-done | bytes 200736 | tf_op jit(solution)/shard_map/ppermute | solution.py:216
  29.4 5.4 %collective-permute-done.2.refs_2_ = bf16[112,896]{1,0:T(8,128)(2,1)S(1)} collective-permute-done((bf16[112,896]{1,0:T(8,128)(2,1)S(1)}, bf16[112,896]{1,0:T(8,128)(2,1)S(1)}, u32[]{:S(2)}, u32[]{:S(2)}) %collective-permute-start.2) | collective-permute-done | bytes 200736 | tf_op jit(solution)/shard_map/ppermute | solution.py:216
  34.8 0.0 collective-permute-done.3.refs_3_
  34.8 0.3 y_sum.1
  35.1 0.0 copy-start.3
  35.1 0.0 copy-start.4
  35.1 3.1 %collective-permute-start.4 = (f32[28,896]{1,0:T(8,128)S(1)}, f32[28,896]{1,0:T(8,128)S(1)}, u32[]{:S(2)}, u32[]{:S(2)}) collective-permute-start(f32[28,896]{1,0:T(8,128)S(1)} %get-tuple-element.30), channel_id=1, source_target_pairs={{0,8},{1,9},{2,10},{3,11},{4,12},{5,13},{6,14},{7,15},{8,16},{9,17... | collective-permute-start | bytes 301064 | tf_op jit(solution)/shard_map/ppermute | solution.py:216
  38.2 2.4 %collective-permute-start.6 = (f32[28,896]{1,0:T(8,128)S(1)}, f32[28,896]{1,0:T(8,128)S(1)}, u32[]{:S(2)}, u32[]{:S(2)}) collective-permute-start(f32[28,896]{1,0:T(8,128)S(1)} %get-tuple-element.32), channel_id=1, source_target_pairs={{0,24},{1,25},{2,26},{3,27},{4,28},{5,29},{6,30},{7,31},{8,0},{9,1... | collective-permute-start | bytes 301064 | tf_op jit(solution)/shard_map/ppermute | solution.py:216
  40.6 4.2 %collective-permute-start.5 = (bf16[28,896]{1,0:T(8,128)(2,1)S(1)}, bf16[28,896]{1,0:T(8,128)(2,1)S(1)}, u32[]{:S(2)}, u32[]{:S(2)}) collective-permute-start(bf16[28,896]{1,0:T(8,128)(2,1)S(1)} %get-tuple-element.31), channel_id=1, source_target_pairs={{0,16},{1,17},{2,18},{3,19},{4,20},{5,21},{6,22},{7,23},{8,24},{9,... | collective-permute-start | bytes 150536 | tf_op jit(solution)/shard_map/ppermute | solution.py:216
  44.8 0.0 all-to-all-done.refs_0_
  44.8 1.7 %update_second.1 = (f32[112,896]{1,0:T(8,128)}, f32[112,896]{1,0:T(8,128)}, bf16[8,112,896]{2,1,0:T(8,128)(2,1)}) custom-call(bf16[8,112,896]{2,1,0:T(8,128)(2,1)S(1)} %all-to-all-done.refs_0_, f32[112,896]{1,0:T(8,128)S(1)} %copy-done.1, f32[112,896]{1,0:T(8,128)S(1)} %copy-done.2, f32[28,896]{1,0:T(8,128)S(1)} %get-tuple-element.29.refs_3_.refs_0_), custom_call_target="tpu_custom_call" | custom-call | bytes 4816896 | tf_op jit(solution)/shard_map/update_second/pallas_call | solution.py:192
  46.5 3.9 %collective-permute-done.5.refs_2_ = bf16[28,896]{1,0:T(8,128)(2,1)S(1)} collective-permute-done((bf16[28,896]{1,0:T(8,128)(2,1)S(1)}, bf16[28,896]{1,0:T(8,128)(2,1)S(1)}, u32[]{:S(2)}, u32[]{:S(2)}) %collective-permute-start.5) | collective-permute-done | bytes 50208 | tf_op jit(solution)/shard_map/ppermute | solution.py:216
  50.4 0.0 collective-permute-done.4.refs_1_
  50.4 0.0 collective-permute-done.6.refs_3_
  50.4 0.7 update_first.1
  51.1 0.8 %collective-permute-start.9 = (bf16[28,896]{1,0:T(8,128)(2,1)S(1)}, bf16[28,896]{1,0:T(8,128)(2,1)S(1)}, u32[]{:S(2)}, u32[]{:S(2)}) collective-permute-start(bf16[28,896]{1,0:T(8,128)(2,1)S(1)} %get-tuple-element.39.refs_0_), channel_id=1, source_target_pairs={{0,24},{1,25},{2,26},{3,27},{4,28},{5,29},{6,30},{7,31},{8,0},{9,1... | collective-permute-start | bytes 150536 | tf_op jit(solution)/shard_map/ppermute | solution.py:216
  52.0 4.7 %collective-permute-start.8 = (bf16[28,896]{1,0:T(8,128)(2,1)S(1)}, bf16[28,896]{1,0:T(8,128)(2,1)S(1)}, u32[]{:S(2)}, u32[]{:S(2)}) collective-permute-start(bf16[28,896]{1,0:T(8,128)(2,1)S(1)} %get-tuple-element.39.refs_0_), channel_id=1, source_target_pairs={{0,16},{1,17},{2,18},{3,19},{4,20},{5,21},{6,22},{7,23},{8,24},{9,... | collective-permute-start | bytes 150536 | tf_op jit(solution)/shard_map/ppermute | solution.py:216
  56.7 0.0 collective-permute-start.7
  56.7 4.1 %all-to-all-start.1 = ((bf16[8,112,896]{2,1,0:T(8,128)(2,1)}), bf16[8,112,896]{2,1,0:T(8,128)(2,1)S(1)}, u32[]{:S(2)}, u32[]{:S(2)}) async-start(bf16[8,112,896]{2,1,0:T(8,128)(2,1)} %get-tuple-element.34.refs_6_), calls=%async_computation.1 | async-start | bytes 3211264 | tf_op jit(solution)/shard_map/all_to_all | solution.py:282
  60.8 0.0 collective-permute-done.9.refs_3_
  60.8 0.0 collective-permute-done.8.refs_2_
  60.8 1.4 %collective-permute-done.7.refs_1_ = bf16[28,896]{1,0:T(8,128)(2,1)S(1)} collective-permute-done((bf16[28,896]{1,0:T(8,128)(2,1)S(1)}, bf16[28,896]{1,0:T(8,128)(2,1)S(1)}, u32[]{:S(2)}, u32[]{:S(2)}) %collective-permute-start.7) | collective-permute-done | bytes 50208 | tf_op jit(solution)/shard_map/ppermute | solution.py:216
  62.2 0.1 join_z.1.refs_0_
  62.3 2.8 %collective-permute-start.12 = (bf16[112,896]{1,0:T(8,128)(2,1)S(1)}, bf16[112,896]{1,0:T(8,128)(2,1)S(1)}, u32[]{:S(2)}, u32[]{:S(2)}) collective-permute-start(bf16[112,896]{1,0:T(8,128)(2,1)S(1)} %join_z.1.refs_0_), channel_id=1, source_target_pairs={{0,6},{1,7},{2,0},{3,1},{4,2},{5,3},{6,4},{7,5},{8,14},{9,15},{10,... | collective-permute-start | bytes 602120 | tf_op jit(solution)/shard_map/ppermute | solution.py:216
  65.1 0.7 collective-permute-start.11
  65.7 0.4 collective-permute-start.10
  66.1 3.9 %collective-permute-start.13 = (bf16[112,896]{1,0:T(8,128)(2,1)S(1)}, bf16[112,896]{1,0:T(8,128)(2,1)S(1)}, u32[]{:S(2)}, u32[]{:S(2)}) collective-permute-start(bf16[112,896]{1,0:T(8,128)(2,1)S(1)} %join_z.1.refs_0_), channel_id=1, source_target_pairs={{0,1},{1,0},{2,3},{3,2},{4,5},{5,4},{6,7},{7,6},{8,9},{9,8},{10,11... | collective-permute-start | bytes 602120 | tf_op jit(solution)/shard_map/ppermute | solution.py:216
  70.1 0.9 %collective-permute-done.12.refs_3_ = bf16[112,896]{1,0:T(8,128)(2,1)S(1)} collective-permute-done((bf16[112,896]{1,0:T(8,128)(2,1)S(1)}, bf16[112,896]{1,0:T(8,128)(2,1)S(1)}, u32[]{:S(2)}, u32[]{:S(2)}) %collective-permute-start.12) | collective-permute-done | bytes 200736 | tf_op jit(solution)/shard_map/ppermute | solution.py:216
  70.9 3.7 %collective-permute-start.16 = (bf16[112,896]{1,0:T(8,128)(2,1)S(1)}, bf16[112,896]{1,0:T(8,128)(2,1)S(1)}, u32[]{:S(2)}, u32[]{:S(2)}) collective-permute-start(bf16[112,896]{1,0:T(8,128)(2,1)S(1)} %collective-permute-done.12.refs_3_), channel_id=1, source_target_pairs={{0,1},{1,0},{2,3},{3,2},{4,5},{5,4},{6,7},{7,6},{8,9},{9,8},{10,11... | collective-permute-start | bytes 602120 | tf_op jit(solution)/shard_map/ppermute | solution.py:216
  74.6 0.0 collective-permute-done.11.refs_2_
  74.6 1.6 %collective-permute-start.15 = (bf16[112,896]{1,0:T(8,128)(2,1)S(1)}, bf16[112,896]{1,0:T(8,128)(2,1)S(1)}, u32[]{:S(2)}, u32[]{:S(2)}) collective-permute-start(bf16[112,896]{1,0:T(8,128)(2,1)S(1)} %collective-permute-done.11.refs_2_), channel_id=1, source_target_pairs={{0,1},{1,0},{2,3},{3,2},{4,5},{5,4},{6,7},{7,6},{8,9},{9,8},{10,11... | collective-permute-start | bytes 602120 | tf_op jit(solution)/shard_map/ppermute | solution.py:216
  76.2 0.4 collective-permute-done.10.refs_1_
  76.6 1.7 %collective-permute-start.14 = (bf16[112,896]{1,0:T(8,128)(2,1)S(1)}, bf16[112,896]{1,0:T(8,128)(2,1)S(1)}, u32[]{:S(2)}, u32[]{:S(2)}) collective-permute-start(bf16[112,896]{1,0:T(8,128)(2,1)S(1)} %collective-permute-done.10.refs_1_), channel_id=1, source_target_pairs={{0,1},{1,0},{2,3},{3,2},{4,5},{5,4},{6,7},{7,6},{8,9},{9,8},{10,11... | collective-permute-start | bytes 602120 | tf_op jit(solution)/shard_map/ppermute | solution.py:216
  78.3 0.0 collective-permute-done.13.refs_4_
  78.3 0.0 collective-permute-done.16.refs_7_
  78.3 0.0 collective-permute-done.15.refs_6_
  78.3 1.1 %collective-permute-done.14.refs_5_ = bf16[112,896]{1,0:T(8,128)(2,1)S(1)} collective-permute-done((bf16[112,896]{1,0:T(8,128)(2,1)S(1)}, bf16[112,896]{1,0:T(8,128)(2,1)S(1)}, u32[]{:S(2)}, u32[]{:S(2)}) %collective-permute-start.14) | collective-permute-done | bytes 200736 | tf_op jit(solution)/shard_map/ppermute | solution.py:216
  79.3 2.2 %join.1 = bf16[896,896]{1,0:T(8,128)(2,1)} custom-call(bf16[112,896]{1,0:T(8,128)(2,1)S(1)} %join_z.1.refs_0_, bf16[112,896]{1,0:T(8,128)(2,1)S(1)} %collective-permute-done.10.refs_1_, bf16[112,896]{1,0:T(8,128)(2,1)S(1)} %collective-permute-done.11.refs_2_, bf16[112,896]{1,0:T(8,128)(2,1)S(1)} %collective-permute-done.12.refs_3_, ...), custom_call_target="tpu_custom_call" | custom-call | bytes 3211264 | tf_op jit(solution)/shard_map/join/pallas_call | solution.py:192
  81.5 0.0 all-to-all-done.1
  81.5 1.2 %copy.15 = bf16[896,896]{1,0:T(8,128)(2,1)} copy(bf16[896,896]{1,0:T(8,128)(2,1)S(1)} %bitcast.2) | data formatting | bytes 3211264
  (8 shorter events, 0.0 us)
Async XLA Ops:
  13.0 7.1 %collective-permute-start = (f32[448,896]{1,0:T(8,128)}, f32[448,896]{1,0:T(8,128)}, u32[]{:S(2)}, u32[]{:S(2)}) collective-permute-start(f32[448,896]{1,0:T(8,128)} %get-tuple-element.24), channel_id=1, source_target_pairs={{0,1},{1,0},{2,3},{3,2},{4,5},{5,4},{6,7},{7,6},{8,9},{9,8},{10,11... | collective-permute-start | bytes 4816904 | tf_op jit(solution)/shard_map/ppermute | solution.py:216
  16.3 3.8 %copy-start = (f32[448,896]{1,0:T(8,128)S(1)}, f32[448,896]{1,0:T(8,128)}, u32[]{:S(2)}) copy-start(f32[448,896]{1,0:T(8,128)} %get-tuple-element.23.refs_0_) | copy-start | bytes 4816900
  16.3 28.5 %all-to-all-start = ((bf16[8,112,896]{2,1,0:T(8,128)(2,1)}), bf16[8,112,896]{2,1,0:T(8,128)(2,1)S(1)}, u32[]{:S(2)}, u32[]{:S(2)}) async-start(bf16[8,112,896]{2,1,0:T(8,128)(2,1)} %bitcast.3), calls=%async_computation | async-start | bytes 3211264 | tf_op jit(solution)/shard_map/all_to_all | solution.py:241
  21.7 7.7 %collective-permute-start.1 = (bf16[112,896]{1,0:T(8,128)(2,1)S(1)}, bf16[112,896]{1,0:T(8,128)(2,1)S(1)}, u32[]{:S(2)}, u32[]{:S(2)}) collective-permute-start(bf16[112,896]{1,0:T(8,128)(2,1)S(1)} %get-tuple-element.26), channel_id=1, source_target_pairs={{0,2},{1,3},{2,4},{3,5},{4,6},{5,7},{6,0},{7,1},{8,10},{9,11},{10,... | collective-permute-start | bytes 602120 | tf_op jit(solution)/shard_map/ppermute | solution.py:216
  23.1 11.7 %collective-permute-start.2 = (bf16[112,896]{1,0:T(8,128)(2,1)S(1)}, bf16[112,896]{1,0:T(8,128)(2,1)S(1)}, u32[]{:S(2)}, u32[]{:S(2)}) collective-permute-start(bf16[112,896]{1,0:T(8,128)(2,1)S(1)} %get-tuple-element.27), channel_id=1, source_target_pairs={{0,4},{1,5},{2,6},{3,7},{4,0},{5,1},{6,2},{7,3},{8,12},{9,13},{10,... | collective-permute-start | bytes 602120 | tf_op jit(solution)/shard_map/ppermute | solution.py:216
  25.7 9.1 %collective-permute-start.3 = (bf16[112,896]{1,0:T(8,128)(2,1)S(1)}, bf16[112,896]{1,0:T(8,128)(2,1)S(1)}, u32[]{:S(2)}, u32[]{:S(2)}) collective-permute-start(bf16[112,896]{1,0:T(8,128)(2,1)S(1)} %get-tuple-element.28), channel_id=1, source_target_pairs={{0,6},{1,7},{2,0},{3,1},{4,2},{5,3},{6,4},{7,5},{8,14},{9,15},{10,... | collective-permute-start | bytes 602120 | tf_op jit(solution)/shard_map/ppermute | solution.py:216
  34.8 10.0 %copy-start.1 = (f32[112,896]{1,0:T(8,128)S(1)}, f32[112,896]{1,0:T(8,128)}, u32[]{:S(2)}) copy-start(f32[112,896]{1,0:T(8,128)} %refs_1_.3) | copy-start | bytes 1204228
  34.8 10.0 %copy-start.2 = (f32[112,896]{1,0:T(8,128)S(1)}, f32[112,896]{1,0:T(8,128)}, u32[]{:S(2)}) copy-start(f32[112,896]{1,0:T(8,128)} %refs_2_.3) | copy-start | bytes 1204228
  35.1 15.3 %copy-start.3 = (f32[28,896]{1,0:T(8,128)S(1)}, f32[28,896]{1,0:T(8,128)}, u32[]{:S(2)}) copy-start(f32[28,896]{1,0:T(8,128)} %refs_4_.1) | copy-start | bytes 301060
  35.1 15.3 %copy-start.4 = (f32[28,896]{1,0:T(8,128)S(1)}, f32[28,896]{1,0:T(8,128)}, u32[]{:S(2)}) copy-start(f32[28,896]{1,0:T(8,128)} %refs_5_.1) | copy-start | bytes 301060
  35.1 15.3 %collective-permute-start.4 = (f32[28,896]{1,0:T(8,128)S(1)}, f32[28,896]{1,0:T(8,128)S(1)}, u32[]{:S(2)}, u32[]{:S(2)}) collective-permute-start(f32[28,896]{1,0:T(8,128)S(1)} %get-tuple-element.30), channel_id=1, source_target_pairs={{0,8},{1,9},{2,10},{3,11},{4,12},{5,13},{6,14},{7,15},{8,16},{9,17... | collective-permute-start | bytes 301064 | tf_op jit(solution)/shard_map/ppermute | solution.py:216
  38.2 12.2 %collective-permute-start.6 = (f32[28,896]{1,0:T(8,128)S(1)}, f32[28,896]{1,0:T(8,128)S(1)}, u32[]{:S(2)}, u32[]{:S(2)}) collective-permute-start(f32[28,896]{1,0:T(8,128)S(1)} %get-tuple-element.32), channel_id=1, source_target_pairs={{0,24},{1,25},{2,26},{3,27},{4,28},{5,29},{6,30},{7,31},{8,0},{9,1... | collective-permute-start | bytes 301064 | tf_op jit(solution)/shard_map/ppermute | solution.py:216
  40.6 9.8 %collective-permute-start.5 = (bf16[28,896]{1,0:T(8,128)(2,1)S(1)}, bf16[28,896]{1,0:T(8,128)(2,1)S(1)}, u32[]{:S(2)}, u32[]{:S(2)}) collective-permute-start(bf16[28,896]{1,0:T(8,128)(2,1)S(1)} %get-tuple-element.31), channel_id=1, source_target_pairs={{0,16},{1,17},{2,18},{3,19},{4,20},{5,21},{6,22},{7,23},{8,24},{9,... | collective-permute-start | bytes 150536 | tf_op jit(solution)/shard_map/ppermute | solution.py:216
  51.1 9.7 %collective-permute-start.9 = (bf16[28,896]{1,0:T(8,128)(2,1)S(1)}, bf16[28,896]{1,0:T(8,128)(2,1)S(1)}, u32[]{:S(2)}, u32[]{:S(2)}) collective-permute-start(bf16[28,896]{1,0:T(8,128)(2,1)S(1)} %get-tuple-element.39.refs_0_), channel_id=1, source_target_pairs={{0,24},{1,25},{2,26},{3,27},{4,28},{5,29},{6,30},{7,31},{8,0},{9,1... | collective-permute-start | bytes 150536 | tf_op jit(solution)/shard_map/ppermute | solution.py:216
  52.0 8.8 %collective-permute-start.8 = (bf16[28,896]{1,0:T(8,128)(2,1)S(1)}, bf16[28,896]{1,0:T(8,128)(2,1)S(1)}, u32[]{:S(2)}, u32[]{:S(2)}) collective-permute-start(bf16[28,896]{1,0:T(8,128)(2,1)S(1)} %get-tuple-element.39.refs_0_), channel_id=1, source_target_pairs={{0,16},{1,17},{2,18},{3,19},{4,20},{5,21},{6,22},{7,23},{8,24},{9,... | collective-permute-start | bytes 150536 | tf_op jit(solution)/shard_map/ppermute | solution.py:216
  56.7 5.5 %collective-permute-start.7 = (bf16[28,896]{1,0:T(8,128)(2,1)S(1)}, bf16[28,896]{1,0:T(8,128)(2,1)S(1)}, u32[]{:S(2)}, u32[]{:S(2)}) collective-permute-start(bf16[28,896]{1,0:T(8,128)(2,1)S(1)} %get-tuple-element.39.refs_0_), channel_id=1, source_target_pairs={{0,8},{1,9},{2,10},{3,11},{4,12},{5,13},{6,14},{7,15},{8,16},{9,17... | collective-permute-start | bytes 150536 | tf_op jit(solution)/shard_map/ppermute | solution.py:216
  56.7 24.8 %all-to-all-start.1 = ((bf16[8,112,896]{2,1,0:T(8,128)(2,1)}), bf16[8,112,896]{2,1,0:T(8,128)(2,1)S(1)}, u32[]{:S(2)}, u32[]{:S(2)}) async-start(bf16[8,112,896]{2,1,0:T(8,128)(2,1)} %get-tuple-element.34.refs_6_), calls=%async_computation.1 | async-start | bytes 3211264 | tf_op jit(solution)/shard_map/all_to_all | solution.py:282
  62.3 8.6 %collective-permute-start.12 = (bf16[112,896]{1,0:T(8,128)(2,1)S(1)}, bf16[112,896]{1,0:T(8,128)(2,1)S(1)}, u32[]{:S(2)}, u32[]{:S(2)}) collective-permute-start(bf16[112,896]{1,0:T(8,128)(2,1)S(1)} %join_z.1.refs_0_), channel_id=1, source_target_pairs={{0,6},{1,7},{2,0},{3,1},{4,2},{5,3},{6,4},{7,5},{8,14},{9,15},{10,... | collective-permute-start | bytes 602120 | tf_op jit(solution)/shard_map/ppermute | solution.py:216
  65.1 9.5 %collective-permute-start.11 = (bf16[112,896]{1,0:T(8,128)(2,1)S(1)}, bf16[112,896]{1,0:T(8,128)(2,1)S(1)}, u32[]{:S(2)}, u32[]{:S(2)}) collective-permute-start(bf16[112,896]{1,0:T(8,128)(2,1)S(1)} %join_z.1.refs_0_), channel_id=1, source_target_pairs={{0,4},{1,5},{2,6},{3,7},{4,0},{5,1},{6,2},{7,3},{8,12},{9,13},{10,... | collective-permute-start | bytes 602120 | tf_op jit(solution)/shard_map/ppermute | solution.py:216
  65.7 10.9 %collective-permute-start.10 = (bf16[112,896]{1,0:T(8,128)(2,1)S(1)}, bf16[112,896]{1,0:T(8,128)(2,1)S(1)}, u32[]{:S(2)}, u32[]{:S(2)}) collective-permute-start(bf16[112,896]{1,0:T(8,128)(2,1)S(1)} %join_z.1.refs_0_), channel_id=1, source_target_pairs={{0,2},{1,3},{2,4},{3,5},{4,6},{5,7},{6,0},{7,1},{8,10},{9,11},{10,... | collective-permute-start | bytes 602120 | tf_op jit(solution)/shard_map/ppermute | solution.py:216
  66.1 12.1 %collective-permute-start.13 = (bf16[112,896]{1,0:T(8,128)(2,1)S(1)}, bf16[112,896]{1,0:T(8,128)(2,1)S(1)}, u32[]{:S(2)}, u32[]{:S(2)}) collective-permute-start(bf16[112,896]{1,0:T(8,128)(2,1)S(1)} %join_z.1.refs_0_), channel_id=1, source_target_pairs={{0,1},{1,0},{2,3},{3,2},{4,5},{5,4},{6,7},{7,6},{8,9},{9,8},{10,11... | collective-permute-start | bytes 602120 | tf_op jit(solution)/shard_map/ppermute | solution.py:216
  70.9 7.4 %collective-permute-start.16 = (bf16[112,896]{1,0:T(8,128)(2,1)S(1)}, bf16[112,896]{1,0:T(8,128)(2,1)S(1)}, u32[]{:S(2)}, u32[]{:S(2)}) collective-permute-start(bf16[112,896]{1,0:T(8,128)(2,1)S(1)} %collective-permute-done.12.refs_3_), channel_id=1, source_target_pairs={{0,1},{1,0},{2,3},{3,2},{4,5},{5,4},{6,7},{7,6},{8,9},{9,8},{10,11... | collective-permute-start | bytes 602120 | tf_op jit(solution)/shard_map/ppermute | solution.py:216
  74.6 3.7 %collective-permute-start.15 = (bf16[112,896]{1,0:T(8,128)(2,1)S(1)}, bf16[112,896]{1,0:T(8,128)(2,1)S(1)}, u32[]{:S(2)}, u32[]{:S(2)}) collective-permute-start(bf16[112,896]{1,0:T(8,128)(2,1)S(1)} %collective-permute-done.11.refs_2_), channel_id=1, source_target_pairs={{0,1},{1,0},{2,3},{3,2},{4,5},{5,4},{6,7},{7,6},{8,9},{9,8},{10,11... | collective-permute-start | bytes 602120 | tf_op jit(solution)/shard_map/ppermute | solution.py:216
  76.6 2.7 %collective-permute-start.14 = (bf16[112,896]{1,0:T(8,128)(2,1)S(1)}, bf16[112,896]{1,0:T(8,128)(2,1)S(1)}, u32[]{:S(2)}, u32[]{:S(2)}) collective-permute-start(bf16[112,896]{1,0:T(8,128)(2,1)S(1)} %collective-permute-done.10.refs_1_), channel_id=1, source_target_pairs={{0,1},{1,0},{2,3},{3,2},{4,5},{5,4},{6,7},{7,6},{8,9},{9,8},{10,11... | collective-permute-start | bytes 602120 | tf_op jit(solution)/shard_map/ppermute | solution.py:216

commit v5 on v4

--- a/solution.py
+++ b/solution.py
@@ -17,7 +17,7 @@
 BLK = ZS * SUB
 SUB2 = D // ROWS
 TB = 512
-RB = 448
+RB = 224
 UNIT = 1.0 / float(D) ** 0.5
 VMEM_BYTES = 32 * 2**20
 MOST_VMEM = 60 * 2**20
@@ -246,10 +246,11 @@
         (((BLK, D), F32),) + (((BLK, D), BF16),) * 3,
         name="core_sum",
     )
-    y_terms = [send(s, 0, k + 1, 0) for k, s in enumerate(sends)]
+    far = send(sends[1], 0, 2, 0)
+    y_terms = [send(sends[0], 0, 1, 0), far, send(sends[2], 0, 3, 0)]
     own, *sends = call(
         y_sum_kernel,
-        (own, *y_terms),
+        (own, y_terms[1], y_terms[0], y_terms[2]),
         tuple(((SUB, D), t) for t in (F32, F32, BF16, F32)),
         [pltpu.VMEM((BLK, D), F32)],
         flops=SOME,

time: 83.3 us -> 83.3 us (level)
    all_to_all x1, starting transfers between devices: 4.09 us -> 5.24 us  [on_device(): reset_second = lax.all_to_all(spread, 'row', 0, 0).reshape(D, D)]
  transfers between devices with their start and end apart: 19 -> 19, of which waited for: 7 -> 6; matrix products, arithmetic and copies ran while one was open for 0% -> 0% of each run, Pallas kernels for 7% -> 7%
where the time goes in v5:
time: 83.3 us; the launch traced here: 82.7 us
  starting transfers between devices  46.8 us (56%)
  Pallas kernels  18.8 us (23%)
  waiting for transfers between devices  15.3 us (18%)
  local copies, waits for them, and re-layouts  1.18 us (1%)
    ppermute x17, starting transfers between devices, send(): return lax.ppermute(value, 'col', shift(dz, dy, dc))  37.8 us
    pallas_call x7, Pallas kernels, call(): pl.pallas_call(body, out_shape=shapes, in_specs=[outside if h else inside...  18.8 us
    ppermute x17, waiting for transfers between devices, send(): return lax.ppermute(value, 'col', shift(dz, dy, dc))  15.3 us
    all_to_all x1, starting transfers between devices, on_device(): reset_second = lax.all_to_all(spread, 'row', 0, 0).reshape(D, D)  5.24 us
    all_to_all x1, starting transfers between devices, on_device(): lax.all_to_all(final_second.reshape(ROWS, SUB2, D), 'row', 0, 0)  3.77 us
  transfers between devices with their start and end apart: 19, of which 6 were waited for; matrix products, arithmetic and copies ran while one was open for 0% of the time, Pallas kernels for 7%

profile of v5, /device:TPU:1, one launch (start us, length us, event | category | flops | bytes accessed | tf_op | source)
XLA Modules:
  0.0 82.7 jit_solution(3155476163185499686)
XLA Ops:
  0.6 12.2 %terms.1 = (f32[448,896]{1,0:T(8,128)}, f32[448,896]{1,0:T(8,128)}, bf16[896,896]{1,0:T(8,128)(2,1)}) custom-call(bf16[1024,896]{1,0:T(8,128)(2,1)} %refs_0_.1, bf16[896,896]{1,0:T(8,128)(2,1)} %refs_1_.2, bf16[1024,896]{1,0:T(8,128)(2,1)} %refs_2_.2, bf16[896,896]{1,0:T(8,128)(2,1)} %refs_3_.1), custom_call_target="tpu_custom_call" | custom-call | flops 6576668672 | bytes 11698176 | tf_op jit(solution)/shard_map/terms/pallas_call | solution.py:192
  12.8 3.3 %collective-permute-start = (f32[448,896]{1,0:T(8,128)}, f32[448,896]{1,0:T(8,128)}, u32[]{:S(2)}, u32[]{:S(2)}) collective-permute-start(f32[448,896]{1,0:T(8,128)} %get-tuple-element.24), channel_id=1, source_target_pairs={{0,1},{1,0},{2,3},{3,2},{4,5},{5,4},{6,7},{7,6},{8,9},{9,8},{10,11... | collective-permute-start | bytes 4816904 | tf_op jit(solution)/shard_map/ppermute | solution.py:216
  16.1 3.8 %all-to-all-start = ((bf16[8,112,896]{2,1,0:T(8,128)(2,1)}), bf16[8,112,896]{2,1,0:T(8,128)(2,1)S(1)}, u32[]{:S(2)}, u32[]{:S(2)}) async-start(bf16[8,112,896]{2,1,0:T(8,128)(2,1)} %bitcast.3), calls=%async_computation | async-start | bytes 3211264 | tf_op jit(solution)/shard_map/all_to_all | solution.py:241
  19.9 0.0 collective-permute-done.refs_1_
  19.9 1.6 %core_sum.1 = (f32[112,896]{1,0:T(8,128)S(1)}, bf16[112,896]{1,0:T(8,128)(2,1)S(1)}, bf16[112,896]{1,0:T(8,128)(2,1)S(1)}, bf16[112,896]{1,0:T(8,128)(2,1)S(1)}) custom-call(f32[448,896]{1,0:T(8,128)S(1)} %copy-done, f32[448,896]{1,0:T(8,128)} %collective-permute-done.refs_1_), custom_call_target="tpu_custom_call" | custom-call | bytes 4214784 | tf_op jit(solution)/shard_map/core_sum/pallas_call | solution.py:192
  21.5 3.0 %collective-permute-start.1 = (bf16[112,896]{1,0:T(8,128)(2,1)S(1)}, bf16[112,896]{1,0:T(8,128)(2,1)S(1)}, u32[]{:S(2)}, u32[]{:S(2)}) collective-permute-start(bf16[112,896]{1,0:T(8,128)(2,1)S(1)} %get-tuple-element.26), channel_id=1, source_target_pairs={{0,4},{1,5},{2,6},{3,7},{4,0},{5,1},{6,2},{7,3},{8,12},{9,13},{10,... | collective-permute-start | bytes 602120 | tf_op jit(solution)/shard_map/ppermute | solution.py:216
  24.5 0.4 collective-permute-start.2
  24.9 2.3 %collective-permute-start.3 = (bf16[112,896]{1,0:T(8,128)(2,1)S(1)}, bf16[112,896]{1,0:T(8,128)(2,1)S(1)}, u32[]{:S(2)}, u32[]{:S(2)}) collective-permute-start(bf16[112,896]{1,0:T(8,128)(2,1)S(1)} %get-tuple-element.28), channel_id=1, source_target_pairs={{0,6},{1,7},{2,0},{3,1},{4,2},{5,3},{6,4},{7,5},{8,14},{9,15},{10,... | collective-permute-start | bytes 602120 | tf_op jit(solution)/shard_map/ppermute | solution.py:216
  27.2 2.2 %collective-permute-done.1.refs_1_ = bf16[112,896]{1,0:T(8,128)(2,1)S(1)} collective-permute-done((bf16[112,896]{1,0:T(8,128)(2,1)S(1)}, bf16[112,896]{1,0:T(8,128)(2,1)S(1)}, u32[]{:S(2)}, u32[]{:S(2)}) %collective-permute-start.1) | collective-permute-done | bytes 200736 | tf_op jit(solution)/shard_map/ppermute | solution.py:216
  29.3 4.9 %collective-permute-done.2.refs_2_ = bf16[112,896]{1,0:T(8,128)(2,1)S(1)} collective-permute-done((bf16[112,896]{1,0:T(8,128)(2,1)S(1)}, bf16[112,896]{1,0:T(8,128)(2,1)S(1)}, u32[]{:S(2)}, u32[]{:S(2)}) %collective-permute-start.2) | collective-permute-done | bytes 200736 | tf_op jit(solution)/shard_map/ppermute | solution.py:216
  34.3 0.0 collective-permute-done.3.refs_3_
  34.3 0.3 y_sum.1
  34.6 0.0 copy-start.3
  34.6 0.0 copy-start.4
  34.6 3.3 %collective-permute-start.4 = (f32[28,896]{1,0:T(8,128)S(1)}, f32[28,896]{1,0:T(8,128)S(1)}, u32[]{:S(2)}, u32[]{:S(2)}) collective-permute-start(f32[28,896]{1,0:T(8,128)S(1)} %get-tuple-element.30), channel_id=1, source_target_pairs={{0,8},{1,9},{2,10},{3,11},{4,12},{5,13},{6,14},{7,15},{8,16},{9,17... | collective-permute-start | bytes 301064 | tf_op jit(solution)/shard_map/ppermute | solution.py:216
  37.9 2.2 %collective-permute-start.6 = (f32[28,896]{1,0:T(8,128)S(1)}, f32[28,896]{1,0:T(8,128)S(1)}, u32[]{:S(2)}, u32[]{:S(2)}) collective-permute-start(f32[28,896]{1,0:T(8,128)S(1)} %get-tuple-element.32), channel_id=1, source_target_pairs={{0,24},{1,25},{2,26},{3,27},{4,28},{5,29},{6,30},{7,31},{8,0},{9,1... | collective-permute-start | bytes 301064 | tf_op jit(solution)/shard_map/ppermute | solution.py:216
  40.1 4.4 %collective-permute-start.5 = (bf16[28,896]{1,0:T(8,128)(2,1)S(1)}, bf16[28,896]{1,0:T(8,128)(2,1)S(1)}, u32[]{:S(2)}, u32[]{:S(2)}) collective-permute-start(bf16[28,896]{1,0:T(8,128)(2,1)S(1)} %get-tuple-element.31), channel_id=1, source_target_pairs={{0,16},{1,17},{2,18},{3,19},{4,20},{5,21},{6,22},{7,23},{8,24},{9,... | collective-permute-start | bytes 150536 | tf_op jit(solution)/shard_map/ppermute | solution.py:216
  44.5 0.0 all-to-all-done.refs_0_
  44.5 1.7 %update_second.1 = (f32[112,896]{1,0:T(8,128)}, f32[112,896]{1,0:T(8,128)}, bf16[8,112,896]{2,1,0:T(8,128)(2,1)}) custom-call(bf16[8,112,896]{2,1,0:T(8,128)(2,1)S(1)} %all-to-all-done.refs_0_, f32[112,896]{1,0:T(8,128)S(1)} %copy-done.1, f32[112,896]{1,0:T(8,128)S(1)} %copy-done.2, f32[28,896]{1,0:T(8,128)S(1)} %get-tuple-element.29.refs_3_.refs_0_), custom_call_target="tpu_custom_call" | custom-call | bytes 4816896 | tf_op jit(solution)/shard_map/update_second/pallas_call | solution.py:192
  46.2 4.8 %collective-permute-done.5.refs_2_ = bf16[28,896]{1,0:T(8,128)(2,1)S(1)} collective-permute-done((bf16[28,896]{1,0:T(8,128)(2,1)S(1)}, bf16[28,896]{1,0:T(8,128)(2,1)S(1)}, u32[]{:S(2)}, u32[]{:S(2)}) %collective-permute-start.5) | collective-permute-done | bytes 50208 | tf_op jit(solution)/shard_map/ppermute | solution.py:216
  50.9 0.0 collective-permute-done.4.refs_1_
  50.9 0.0 collective-permute-done.6.refs_3_
  51.0 0.7 update_first.1
  51.7 0.0 collective-permute-start.9
  51.7 4.2 %collective-permute-start.8 = (bf16[28,896]{1,0:T(8,128)(2,1)S(1)}, bf16[28,896]{1,0:T(8,128)(2,1)S(1)}, u32[]{:S(2)}, u32[]{:S(2)}) collective-permute-start(bf16[28,896]{1,0:T(8,128)(2,1)S(1)} %get-tuple-element.39.refs_0_), channel_id=1, source_target_pairs={{0,16},{1,17},{2,18},{3,19},{4,20},{5,21},{6,22},{7,23},{8,24},{9,... | collective-permute-start | bytes 150536 | tf_op jit(solution)/shard_map/ppermute | solution.py:216
  55.9 0.0 collective-permute-start.7
  55.9 5.2 %all-to-all-start.1 = ((bf16[8,112,896]{2,1,0:T(8,128)(2,1)}), bf16[8,112,896]{2,1,0:T(8,128)(2,1)S(1)}, u32[]{:S(2)}, u32[]{:S(2)}) async-start(bf16[8,112,896]{2,1,0:T(8,128)(2,1)} %get-tuple-element.34.refs_6_), calls=%async_computation.1 | async-start | bytes 3211264 | tf_op jit(solution)/shard_map/all_to_all | solution.py:283
  61.1 0.0 collective-permute-done.9.refs_3_
  61.1 0.0 collective-permute-done.8.refs_2_
  61.1 1.2 %collective-permute-done.7.refs_1_ = bf16[28,896]{1,0:T(8,128)(2,1)S(1)} collective-permute-done((bf16[28,896]{1,0:T(8,128)(2,1)S(1)}, bf16[28,896]{1,0:T(8,128)(2,1)S(1)}, u32[]{:S(2)}, u32[]{:S(2)}) %collective-permute-start.7) | collective-permute-done | bytes 50208 | tf_op jit(solution)/shard_map/ppermute | solution.py:216
  62.4 0.1 join_z.1.refs_0_
  62.5 2.6 %collective-permute-start.12 = (bf16[112,896]{1,0:T(8,128)(2,1)S(1)}, bf16[112,896]{1,0:T(8,128)(2,1)S(1)}, u32[]{:S(2)}, u32[]{:S(2)}) collective-permute-start(bf16[112,896]{1,0:T(8,128)(2,1)S(1)} %join_z.1.refs_0_), channel_id=1, source_target_pairs={{0,6},{1,7},{2,0},{3,1},{4,2},{5,3},{6,4},{7,5},{8,14},{9,15},{10,... | collective-permute-start | bytes 602120 | tf_op jit(solution)/shard_map/ppermute | solution.py:216
  65.1 1.5 %collective-permute-start.11 = (bf16[112,896]{1,0:T(8,128)(2,1)S(1)}, bf16[112,896]{1,0:T(8,128)(2,1)S(1)}, u32[]{:S(2)}, u32[]{:S(2)}) collective-permute-start(bf16[112,896]{1,0:T(8,128)(2,1)S(1)} %join_z.1.refs_0_), channel_id=1, source_target_pairs={{0,4},{1,5},{2,6},{3,7},{4,0},{5,1},{6,2},{7,3},{8,12},{9,13},{10,... | collective-permute-start | bytes 602120 | tf_op jit(solution)/shard_map/ppermute | solution.py:216
  66.7 0.8 collective-permute-start.10
  67.4 1.9 %collective-permute-start.13 = (bf16[112,896]{1,0:T(8,128)(2,1)S(1)}, bf16[112,896]{1,0:T(8,128)(2,1)S(1)}, u32[]{:S(2)}, u32[]{:S(2)}) collective-permute-start(bf16[112,896]{1,0:T(8,128)(2,1)S(1)} %join_z.1.refs_0_), channel_id=1, source_target_pairs={{0,1},{1,0},{2,3},{3,2},{4,5},{5,4},{6,7},{7,6},{8,9},{9,8},{10,11... | collective-permute-start | bytes 602120 | tf_op jit(solution)/shard_map/ppermute | solution.py:216
  69.4 0.0 collective-permute-done.12.refs_3_
  69.4 5.3 %collective-permute-start.16 = (bf16[112,896]{1,0:T(8,128)(2,1)S(1)}, bf16[112,896]{1,0:T(8,128)(2,1)S(1)}, u32[]{:S(2)}, u32[]{:S(2)}) collective-permute-start(bf16[112,896]{1,0:T(8,128)(2,1)S(1)} %collective-permute-done.12.refs_3_), channel_id=1, source_target_pairs={{0,1},{1,0},{2,3},{3,2},{4,5},{5,4},{6,7},{7,6},{8,9},{9,8},{10,11... | collective-permute-start | bytes 602120 | tf_op jit(solution)/shard_map/ppermute | solution.py:216
  74.7 0.0 collective-permute-done.11.refs_2_
  74.7 1.5 %collective-permute-start.15 = (bf16[112,896]{1,0:T(8,128)(2,1)S(1)}, bf16[112,896]{1,0:T(8,128)(2,1)S(1)}, u32[]{:S(2)}, u32[]{:S(2)}) collective-permute-start(bf16[112,896]{1,0:T(8,128)(2,1)S(1)} %collective-permute-done.11.refs_2_), channel_id=1, source_target_pairs={{0,1},{1,0},{2,3},{3,2},{4,5},{5,4},{6,7},{7,6},{8,9},{9,8},{10,11... | collective-permute-start | bytes 602120 | tf_op jit(solution)/shard_map/ppermute | solution.py:216
  76.2 1.1 %collective-permute-done.10.refs_1_ = bf16[112,896]{1,0:T(8,128)(2,1)S(1)} collective-permute-done((bf16[112,896]{1,0:T(8,128)(2,1)S(1)}, bf16[112,896]{1,0:T(8,128)(2,1)S(1)}, u32[]{:S(2)}, u32[]{:S(2)}) %collective-permute-start.10) | collective-permute-done | bytes 200736 | tf_op jit(solution)/shard_map/ppermute | solution.py:216
  77.3 1.1 %collective-permute-start.14 = (bf16[112,896]{1,0:T(8,128)(2,1)S(1)}, bf16[112,896]{1,0:T(8,128)(2,1)S(1)}, u32[]{:S(2)}, u32[]{:S(2)}) collective-permute-start(bf16[112,896]{1,0:T(8,128)(2,1)S(1)} %collective-permute-done.10.refs_1_), channel_id=1, source_target_pairs={{0,1},{1,0},{2,3},{3,2},{4,5},{5,4},{6,7},{7,6},{8,9},{9,8},{10,11... | collective-permute-start | bytes 602120 | tf_op jit(solution)/shard_map/ppermute | solution.py:216
  78.3 0.0 collective-permute-done.13.refs_4_
  78.3 0.0 collective-permute-done.16.refs_7_
  78.3 0.0 collective-permute-done.15.refs_6_
  78.3 1.1 %collective-permute-done.14.refs_5_ = bf16[112,896]{1,0:T(8,128)(2,1)S(1)} collective-permute-done((bf16[112,896]{1,0:T(8,128)(2,1)S(1)}, bf16[112,896]{1,0:T(8,128)(2,1)S(1)}, u32[]{:S(2)}, u32[]{:S(2)}) %collective-permute-start.14) | collective-permute-done | bytes 200736 | tf_op jit(solution)/shard_map/ppermute | solution.py:216
  79.4 2.2 %join.1 = bf16[896,896]{1,0:T(8,128)(2,1)} custom-call(bf16[112,896]{1,0:T(8,128)(2,1)S(1)} %join_z.1.refs_0_, bf16[112,896]{1,0:T(8,128)(2,1)S(1)} %collective-permute-done.10.refs_1_, bf16[112,896]{1,0:T(8,128)(2,1)S(1)} %collective-permute-done.11.refs_2_, bf16[112,896]{1,0:T(8,128)(2,1)S(1)} %collective-permute-done.12.refs_3_, ...), custom_call_target="tpu_custom_call" | custom-call | bytes 3211264 | tf_op jit(solution)/shard_map/join/pallas_call | solution.py:192
  81.6 0.0 all-to-all-done.1
  81.6 1.2 %copy.15 = bf16[896,896]{1,0:T(8,128)(2,1)} copy(bf16[896,896]{1,0:T(8,128)(2,1)S(1)} %bitcast.2) | data formatting | bytes 3211264
  (8 shorter events, 0.0 us)
Async XLA Ops:
  12.8 7.1 %collective-permute-start = (f32[448,896]{1,0:T(8,128)}, f32[448,896]{1,0:T(8,128)}, u32[]{:S(2)}, u32[]{:S(2)}) collective-permute-start(f32[448,896]{1,0:T(8,128)} %get-tuple-element.24), channel_id=1, source_target_pairs={{0,1},{1,0},{2,3},{3,2},{4,5},{5,4},{6,7},{7,6},{8,9},{9,8},{10,11... | collective-permute-start | bytes 4816904 | tf_op jit(solution)/shard_map/ppermute | solution.py:216
  16.1 3.8 %copy-start = (f32[448,896]{1,0:T(8,128)S(1)}, f32[448,896]{1,0:T(8,128)}, u32[]{:S(2)}) copy-start(f32[448,896]{1,0:T(8,128)} %get-tuple-element.23.refs_0_) | copy-start | bytes 4816900
  16.1 28.4 %all-to-all-start = ((bf16[8,112,896]{2,1,0:T(8,128)(2,1)}), bf16[8,112,896]{2,1,0:T(8,128)(2,1)S(1)}, u32[]{:S(2)}, u32[]{:S(2)}) async-start(bf16[8,112,896]{2,1,0:T(8,128)(2,1)} %bitcast.3), calls=%async_computation | async-start | bytes 3211264 | tf_op jit(solution)/shard_map/all_to_all | solution.py:241
  21.5 7.9 %collective-permute-start.1 = (bf16[112,896]{1,0:T(8,128)(2,1)S(1)}, bf16[112,896]{1,0:T(8,128)(2,1)S(1)}, u32[]{:S(2)}, u32[]{:S(2)}) collective-permute-start(bf16[112,896]{1,0:T(8,128)(2,1)S(1)} %get-tuple-element.26), channel_id=1, source_target_pairs={{0,4},{1,5},{2,6},{3,7},{4,0},{5,1},{6,2},{7,3},{8,12},{9,13},{10,... | collective-permute-start | bytes 602120 | tf_op jit(solution)/shard_map/ppermute | solution.py:216
  24.5 9.8 %collective-permute-start.2 = (bf16[112,896]{1,0:T(8,128)(2,1)S(1)}, bf16[112,896]{1,0:T(8,128)(2,1)S(1)}, u32[]{:S(2)}, u32[]{:S(2)}) collective-permute-start(bf16[112,896]{1,0:T(8,128)(2,1)S(1)} %get-tuple-element.27), channel_id=1, source_target_pairs={{0,2},{1,3},{2,4},{3,5},{4,6},{5,7},{6,0},{7,1},{8,10},{9,11},{10,... | collective-permute-start | bytes 602120 | tf_op jit(solution)/shard_map/ppermute | solution.py:216
  24.9 9.4 %collective-permute-start.3 = (bf16[112,896]{1,0:T(8,128)(2,1)S(1)}, bf16[112,896]{1,0:T(8,128)(2,1)S(1)}, u32[]{:S(2)}, u32[]{:S(2)}) collective-permute-start(bf16[112,896]{1,0:T(8,128)(2,1)S(1)} %get-tuple-element.28), channel_id=1, source_target_pairs={{0,6},{1,7},{2,0},{3,1},{4,2},{5,3},{6,4},{7,5},{8,14},{9,15},{10,... | collective-permute-start | bytes 602120 | tf_op jit(solution)/shard_map/ppermute | solution.py:216
  34.3 10.2 %copy-start.1 = (f32[112,896]{1,0:T(8,128)S(1)}, f32[112,896]{1,0:T(8,128)}, u32[]{:S(2)}) copy-start(f32[112,896]{1,0:T(8,128)} %refs_1_.3) | copy-start | bytes 1204228
  34.3 10.2 %copy-start.2 = (f32[112,896]{1,0:T(8,128)S(1)}, f32[112,896]{1,0:T(8,128)}, u32[]{:S(2)}) copy-start(f32[112,896]{1,0:T(8,128)} %refs_2_.3) | copy-start | bytes 1204228
  34.6 16.3 %copy-start.3 = (f32[28,896]{1,0:T(8,128)S(1)}, f32[28,896]{1,0:T(8,128)}, u32[]{:S(2)}) copy-start(f32[28,896]{1,0:T(8,128)} %refs_4_.1) | copy-start | bytes 301060
  34.6 16.3 %copy-start.4 = (f32[28,896]{1,0:T(8,128)S(1)}, f32[28,896]{1,0:T(8,128)}, u32[]{:S(2)}) copy-start(f32[28,896]{1,0:T(8,128)} %refs_5_.1) | copy-start | bytes 301060
  34.6 16.3 %collective-permute-start.4 = (f32[28,896]{1,0:T(8,128)S(1)}, f32[28,896]{1,0:T(8,128)S(1)}, u32[]{:S(2)}, u32[]{:S(2)}) collective-permute-start(f32[28,896]{1,0:T(8,128)S(1)} %get-tuple-element.30), channel_id=1, source_target_pairs={{0,8},{1,9},{2,10},{3,11},{4,12},{5,13},{6,14},{7,15},{8,16},{9,17... | collective-permute-start | bytes 301064 | tf_op jit(solution)/shard_map/ppermute | solution.py:216
  37.9 13.1 %collective-permute-start.6 = (f32[28,896]{1,0:T(8,128)S(1)}, f32[28,896]{1,0:T(8,128)S(1)}, u32[]{:S(2)}, u32[]{:S(2)}) collective-permute-start(f32[28,896]{1,0:T(8,128)S(1)} %get-tuple-element.32), channel_id=1, source_target_pairs={{0,24},{1,25},{2,26},{3,27},{4,28},{5,29},{6,30},{7,31},{8,0},{9,1... | collective-permute-start | bytes 301064 | tf_op jit(solution)/shard_map/ppermute | solution.py:216
  40.1 10.8 %collective-permute-start.5 = (bf16[28,896]{1,0:T(8,128)(2,1)S(1)}, bf16[28,896]{1,0:T(8,128)(2,1)S(1)}, u32[]{:S(2)}, u32[]{:S(2)}) collective-permute-start(bf16[28,896]{1,0:T(8,128)(2,1)S(1)} %get-tuple-element.31), channel_id=1, source_target_pairs={{0,16},{1,17},{2,18},{3,19},{4,20},{5,21},{6,22},{7,23},{8,24},{9,... | collective-permute-start | bytes 150536 | tf_op jit(solution)/shard_map/ppermute | solution.py:216
  51.7 9.4 %collective-permute-start.9 = (bf16[28,896]{1,0:T(8,128)(2,1)S(1)}, bf16[28,896]{1,0:T(8,128)(2,1)S(1)}, u32[]{:S(2)}, u32[]{:S(2)}) collective-permute-start(bf16[28,896]{1,0:T(8,128)(2,1)S(1)} %get-tuple-element.39.refs_0_), channel_id=1, source_target_pairs={{0,24},{1,25},{2,26},{3,27},{4,28},{5,29},{6,30},{7,31},{8,0},{9,1... | collective-permute-start | bytes 150536 | tf_op jit(solution)/shard_map/ppermute | solution.py:216
  51.7 9.4 %collective-permute-start.8 = (bf16[28,896]{1,0:T(8,128)(2,1)S(1)}, bf16[28,896]{1,0:T(8,128)(2,1)S(1)}, u32[]{:S(2)}, u32[]{:S(2)}) collective-permute-start(bf16[28,896]{1,0:T(8,128)(2,1)S(1)} %get-tuple-element.39.refs_0_), channel_id=1, source_target_pairs={{0,16},{1,17},{2,18},{3,19},{4,20},{5,21},{6,22},{7,23},{8,24},{9,... | collective-permute-start | bytes 150536 | tf_op jit(solution)/shard_map/ppermute | solution.py:216
  55.9 6.5 %collective-permute-start.7 = (bf16[28,896]{1,0:T(8,128)(2,1)S(1)}, bf16[28,896]{1,0:T(8,128)(2,1)S(1)}, u32[]{:S(2)}, u32[]{:S(2)}) collective-permute-start(bf16[28,896]{1,0:T(8,128)(2,1)S(1)} %get-tuple-element.39.refs_0_), channel_id=1, source_target_pairs={{0,8},{1,9},{2,10},{3,11},{4,12},{5,13},{6,14},{7,15},{8,16},{9,17... | collective-permute-start | bytes 150536 | tf_op jit(solution)/shard_map/ppermute | solution.py:216
  55.9 25.7 %all-to-all-start.1 = ((bf16[8,112,896]{2,1,0:T(8,128)(2,1)}), bf16[8,112,896]{2,1,0:T(8,128)(2,1)S(1)}, u32[]{:S(2)}, u32[]{:S(2)}) async-start(bf16[8,112,896]{2,1,0:T(8,128)(2,1)} %get-tuple-element.34.refs_6_), calls=%async_computation.1 | async-start | bytes 3211264 | tf_op jit(solution)/shard_map/all_to_all | solution.py:283
  62.5 6.9 %collective-permute-start.12 = (bf16[112,896]{1,0:T(8,128)(2,1)S(1)}, bf16[112,896]{1,0:T(8,128)(2,1)S(1)}, u32[]{:S(2)}, u32[]{:S(2)}) collective-permute-start(bf16[112,896]{1,0:T(8,128)(2,1)S(1)} %join_z.1.refs_0_), channel_id=1, source_target_pairs={{0,6},{1,7},{2,0},{3,1},{4,2},{5,3},{6,4},{7,5},{8,14},{9,15},{10,... | collective-permute-start | bytes 602120 | tf_op jit(solution)/shard_map/ppermute | solution.py:216
  65.1 9.5 %collective-permute-start.11 = (bf16[112,896]{1,0:T(8,128)(2,1)S(1)}, bf16[112,896]{1,0:T(8,128)(2,1)S(1)}, u32[]{:S(2)}, u32[]{:S(2)}) collective-permute-start(bf16[112,896]{1,0:T(8,128)(2,1)S(1)} %join_z.1.refs_0_), channel_id=1, source_target_pairs={{0,4},{1,5},{2,6},{3,7},{4,0},{5,1},{6,2},{7,3},{8,12},{9,13},{10,... | collective-permute-start | bytes 602120 | tf_op jit(solution)/shard_map/ppermute | solution.py:216
  66.7 10.6 %collective-permute-start.10 = (bf16[112,896]{1,0:T(8,128)(2,1)S(1)}, bf16[112,896]{1,0:T(8,128)(2,1)S(1)}, u32[]{:S(2)}, u32[]{:S(2)}) collective-permute-start(bf16[112,896]{1,0:T(8,128)(2,1)S(1)} %join_z.1.refs_0_), channel_id=1, source_target_pairs={{0,2},{1,3},{2,4},{3,5},{4,6},{5,7},{6,0},{7,1},{8,10},{9,11},{10,... | collective-permute-start | bytes 602120 | tf_op jit(solution)/shard_map/ppermute | solution.py:216
  67.4 10.9 %collective-permute-start.13 = (bf16[112,896]{1,0:T(8,128)(2,1)S(1)}, bf16[112,896]{1,0:T(8,128)(2,1)S(1)}, u32[]{:S(2)}, u32[]{:S(2)}) collective-permute-start(bf16[112,896]{1,0:T(8,128)(2,1)S(1)} %join_z.1.refs_0_), channel_id=1, source_target_pairs={{0,1},{1,0},{2,3},{3,2},{4,5},{5,4},{6,7},{7,6},{8,9},{9,8},{10,11... | collective-permute-start | bytes 602120 | tf_op jit(solution)/shard_map/ppermute | solution.py:216
  69.4 9.0 %collective-permute-start.16 = (bf16[112,896]{1,0:T(8,128)(2,1)S(1)}, bf16[112,896]{1,0:T(8,128)(2,1)S(1)}, u32[]{:S(2)}, u32[]{:S(2)}) collective-permute-start(bf16[112,896]{1,0:T(8,128)(2,1)S(1)} %collective-permute-done.12.refs_3_), channel_id=1, source_target_pairs={{0,1},{1,0},{2,3},{3,2},{4,5},{5,4},{6,7},{7,6},{8,9},{9,8},{10,11... | collective-permute-start | bytes 602120 | tf_op jit(solution)/shard_map/ppermute | solution.py:216
  74.7 3.7 %collective-permute-start.15 = (bf16[112,896]{1,0:T(8,128)(2,1)S(1)}, bf16[112,896]{1,0:T(8,128)(2,1)S(1)}, u32[]{:S(2)}, u32[]{:S(2)}) collective-permute-start(bf16[112,896]{1,0:T(8,128)(2,1)S(1)} %collective-permute-done.11.refs_2_), channel_id=1, source_target_pairs={{0,1},{1,0},{2,3},{3,2},{4,5},{5,4},{6,7},{7,6},{8,9},{9,8},{10,11... | collective-permute-start | bytes 602120 | tf_op jit(solution)/shard_map/ppermute | solution.py:216
  77.3 2.1 %collective-permute-start.14 = (bf16[112,896]{1,0:T(8,128)(2,1)S(1)}, bf16[112,896]{1,0:T(8,128)(2,1)S(1)}, u32[]{:S(2)}, u32[]{:S(2)}) collective-permute-start(bf16[112,896]{1,0:T(8,128)(2,1)S(1)} %collective-permute-done.10.refs_1_), channel_id=1, source_target_pairs={{0,1},{1,0},{2,3},{3,2},{4,5},{5,4},{6,7},{7,6},{8,9},{9,8},{10,11... | collective-permute-start | bytes 602120 | tf_op jit(solution)/shard_map/ppermute | solution.py:216
